TPU v7x, 128 devices: a whole 4x4x4 slice. The times are simulated.
128 devices in a mesh: section: 2 (over y_hi), shard: 8 (over x, core), replica: 8 (over z, y_lo).
Axes of the slice: x: 4, y: 4 (y_hi: 2, y_lo: 2; y = y_hi * 2 + y_lo), z: 4, core: 2. Of those that a mesh axis runs over, the one named last changes fastest.
Arguments:
- boundary: bfloat16 [2, 2, 8, 768, 1024], P('section', None, 'replica', 'shard'), may hold values from -6 to 6
- image_of_token: int32 [2, 8, 768], P(None, 'replica'), may hold values from 0 to 2, as said below
- ln1_gain: bfloat16 [2, 1024], P('section', 'shard'), may hold values from 0.5 to 1.5
- ln1_bias: bfloat16 [2, 1024], P('section', 'shard'), may hold values from -1.25 to 1.25
- w_qkv: bfloat16 [2, 1024, 3072], P('section', 'shard'), may hold values from -0.1875 to 0.1875
- qv_bias: bfloat16 [2, 2048], P('section', 'shard'), may hold values from -1.25 to 1.25
- w_out: bfloat16 [2, 1024, 1024], P('section', 'shard'), may hold values from -3 to 3
- out_bias: bfloat16 [2, 1024], P('section', 'shard'), may hold values from -1.25 to 1.25
- ln2_gain: bfloat16 [2, 1024], P('section', 'shard'), may hold values from 0.5 to 1.5
- ln2_bias: bfloat16 [2, 1024], P('section', 'shard'), may hold values from -1.25 to 1.25
- w_fc1: bfloat16 [2, 1024, 4096], P('section', 'shard'), may hold values from -0.1875 to 0.1875
- fc1_bias: bfloat16 [2, 4096], P('section', 'shard'), may hold values from -1.25 to 1.25
- w_fc2: bfloat16 [2, 4096, 1024], P('section', 'shard'), may hold values from -0.09375 to 0.09375
- fc2_bias: bfloat16 [2, 1024], P('section', 'shard'), may hold values from -1.25 to 1.25
Outputs:
- boundary_out: float32 [2, 2, 8, 768, 1024], P('section', None, 'replica', 'shard')
- grad_ln1_gain: float32 [2, 1024], P('section', 'shard')
- grad_ln1_bias: float32 [2, 1024], P('section', 'shard')
- grad_w_qkv: float32 [2, 1024, 3072], P('section', 'shard')
- grad_qv_bias: float32 [2, 2048], P('section', 'shard')
- grad_w_out: float32 [2, 1024, 1024], P('section', 'shard')
- grad_out_bias: float32 [2, 1024], P('section', 'shard')
- grad_ln2_gain: float32 [2, 1024], P('section', 'shard')
- grad_ln2_bias: float32 [2, 1024], P('section', 'shard')
- grad_w_fc1: float32 [2, 1024, 4096], P('section', 'shard')
- grad_fc1_bias: float32 [2, 4096], P('section', 'shard')
- grad_w_fc2: float32 [2, 4096, 1024], P('section', 'shard')
- grad_fc2_bias: float32 [2, 1024], P('section', 'shard')
Inputs may be any that keep to these rules, and one draw needn't show every extreme that they name: `image_of_token`: in every pack the image numbers start at 0, never fall and rise by one at each new image; every image of a pack but its first and its last has exactly 577 tokens, and those two have 1 to 577 tokens.
All inputs are finite; a program needn't handle non-finite values.
Results may differ from a plain program's by a relative error of at most 0.014.
Values may be sent and summed in bfloat16 or wider, within the bound.
A program may use at most 192 MiB of HBM per device.

v0:
```python
import math

import jax
import jax.numpy as jnp
from jax import lax
from jax.sharding import PartitionSpec as P

D = 1024
HEADS = 16
HEAD = 64


EPS = 1e-06
NEG = -1e30


def from_behind(x, axis, by):
    devices = lax.axis_size(axis)
    pairs = [(i, i + by) for i in range(devices) if 0 <= i + by < devices]
    return lax.ppermute(x, axis, pairs)


def layer_norm(resid_in, gain_vec, offset):
    centered = resid_in - jnp.mean(resid_in, axis=-1, keepdims=True)
    variance = jnp.mean(centered * centered, axis=-1, keepdims=True)
    return centered * lax.rsqrt(variance + EPS) * gain_vec + offset


def gelu_exact(inputs):
    return jax.nn.gelu(inputs, approximate=False)


def matmul(first_op, second_op):
    return jnp.dot(first_op, second_op, preferred_element_type=jnp.float32)


def matmul_t(first_op, second_op):
    return lax.dot_general(
        first_op, second_op, (((1,), (1,)), ((), ())), preferred_element_type=jnp.float32
    )


def over_rows(first_op, second_op):
    return lax.dot_general(
        first_op, second_op, (((0,), (0,)), ((), ())), preferred_element_type=jnp.float32
    )


def by_heads(matrix):
    return matrix.reshape(matrix.shape[0], HEADS, HEAD)


def masked_scores(queries, key_rows, query_ids, key_ids):
    scores = jnp.einsum(
        "qhd,khd->hqk", by_heads(queries), by_heads(key_rows), preferred_element_type=jnp.float32
    )
    scores = scores * (1.0 / math.sqrt(HEAD))
    allowed = (query_ids[:, None] == key_ids[None, :])[None]
    return jnp.where(allowed, scores, NEG)


def forward_block(weights, resid_in, image_ids, start_row):
    (
        ln1_gain,
        ln1_bias,
        w_qkv,
        qv_bias,
        w_out,
        out_bias,
        ln2_gain,
        ln2_bias,
        w_fc1,
        fc1_bias,
        w_fc2,
        fc2_bias,
    ) = weights
    token_count = resid_in.shape[0]
    query_ids = lax.dynamic_slice_in_dim(image_ids, start_row, token_count)
    normed_one = layer_norm(resid_in, ln1_gain, ln1_bias).astype(jnp.bfloat16)
    bias_full = jnp.concatenate([qv_bias[:D], jnp.zeros((D,), jnp.float32), qv_bias[D:]])
    projected = (matmul(normed_one, w_qkv) + bias_full).astype(jnp.bfloat16)
    kv_full = lax.all_gather(projected[:, D:], "shard", axis=0, tiled=True)
    scores = masked_scores(projected[:, :D], kv_full[:, :D], query_ids, image_ids)
    row_max = jnp.max(scores, axis=-1, keepdims=True)
    shifted = jnp.exp(scores - row_max)
    row_sum = jnp.sum(shifted, axis=-1, keepdims=True)
    probs_low = (shifted / row_sum).astype(jnp.bfloat16)
    log_total = row_max + jnp.log(row_sum)
    weighted = jnp.einsum(
        "hqk,khd->qhd", probs_low, by_heads(kv_full[:, D:]), preferred_element_type=jnp.float32
    )
    weighted = weighted.reshape(token_count, D).astype(jnp.bfloat16)
    resid_mid = resid_in + (matmul(weighted, w_out) + out_bias)
    normed_two = layer_norm(resid_mid, ln2_gain, ln2_bias).astype(jnp.bfloat16)
    hidden = matmul(normed_two, w_fc1) + fc1_bias
    activated = gelu_exact(hidden).astype(jnp.bfloat16)
    resid_out = resid_mid + (matmul(activated, w_fc2) + fc2_bias)
    stored = (
        resid_in,
        normed_one,
        projected,
        kv_full,
        log_total,
        weighted,
        resid_mid,
        normed_two,
        hidden,
        activated,
        image_ids,
    )
    return (resid_out, stored)


def backward_block(weights, stored, grad_out, start_row):
    (
        ln1_gain,
        ln1_bias,
        w_qkv,
        qv_bias,
        w_out,
        out_bias,
        ln2_gain,
        ln2_bias,
        w_fc1,
        fc1_bias,
        w_fc2,
        fc2_bias,
    ) = weights
    (
        resid_in,
        normed_one,
        projected,
        kv_full,
        log_total,
        weighted,
        resid_mid,
        normed_two,
        hidden,
        activated,
        image_ids,
    ) = stored
    token_count = resid_in.shape[0]
    score_scale = 1.0 / math.sqrt(HEAD)
    grad_mlp = grad_out.astype(jnp.bfloat16)
    d_activated = matmul_t(grad_mlp, w_fc2)
    d_hidden = jax.vjp(gelu_exact, hidden)[1](d_activated)[0].astype(jnp.bfloat16)
    d_normed_two = matmul_t(d_hidden, w_fc1)
    d_mid, d_ln2_gain, d_ln2_bias = jax.vjp(layer_norm, resid_mid, ln2_gain, ln2_bias)[1](
        d_normed_two
    )
    d_mid = grad_out + d_mid
    grad_attn = d_mid.astype(jnp.bfloat16)
    d_weighted = matmul_t(grad_attn, w_out).astype(jnp.bfloat16)
    query_ids = lax.dynamic_slice_in_dim(image_ids, start_row, token_count)
    scores = masked_scores(projected[:, :D], kv_full[:, :D], query_ids, image_ids)
    attn_probs = jnp.exp(scores - log_total)
    grad_heads = by_heads(d_weighted)
    query_heads = by_heads(projected[:, :D])
    d_probs = jnp.einsum(
        "qhd,khd->hqk", grad_heads, by_heads(kv_full[:, D:]), preferred_element_type=jnp.float32
    )
    d_scores = (
        attn_probs * (d_probs - jnp.sum(d_probs * attn_probs, axis=-1, keepdims=True))
    ).astype(jnp.bfloat16)
    probs_low = attn_probs.astype(jnp.bfloat16)
    d_queries = jnp.einsum(
        "hqk,khd->qhd", d_scores, by_heads(kv_full[:, :D]), preferred_element_type=jnp.float32
    )
    d_queries = d_queries.reshape(token_count, D) * score_scale
    d_keys = jnp.einsum("hqk,qhd->khd", d_scores, query_heads, preferred_element_type=jnp.float32)
    d_values = jnp.einsum("hqk,qhd->khd", probs_low, grad_heads, preferred_element_type=jnp.float32)
    d_kv = lax.psum_scatter(
        jnp.concatenate(
            [
                d_keys.reshape(token_count * lax.axis_size("shard"), D) * score_scale,
                d_values.reshape(token_count * lax.axis_size("shard"), D),
            ],
            axis=1,
        ).astype(jnp.bfloat16),
        "shard",
        scatter_dimension=0,
        tiled=True,
    ).astype(jnp.float32)
    d_projected = jnp.concatenate([d_queries, d_kv], axis=1).astype(jnp.bfloat16)
    d_normed_one = matmul_t(d_projected, w_qkv)
    d_resid, d_ln1_gain, d_ln1_bias = jax.vjp(layer_norm, resid_in, ln1_gain, ln1_bias)[1](
        d_normed_one
    )
    d_resid = d_mid + d_resid
    proj_wide = d_projected.astype(jnp.float32)
    d_qv_bias = jnp.concatenate(
        [jnp.sum(proj_wide[:, :D], axis=0), jnp.sum(proj_wide[:, 2 * D :], axis=0)]
    )
    vectors = (
        d_ln1_gain,
        d_ln1_bias,
        d_qv_bias,
        jnp.sum(grad_attn.astype(jnp.float32), axis=0),
        d_ln2_gain,
        d_ln2_bias,
        jnp.sum(d_hidden.astype(jnp.float32), axis=0),
        jnp.sum(grad_mlp.astype(jnp.float32), axis=0),
    )
    pair_terms = (
        (normed_one, d_projected),
        (weighted, grad_attn),
        (normed_two, d_hidden),
        (activated, grad_mlp),
    )
    return (d_resid, vectors, pair_terms)


def body(
    boundary,
    image_of_token,
    ln1_gain,
    ln1_bias,
    w_qkv,
    qv_bias,
    w_out,
    out_bias,
    ln2_gain,
    ln2_bias,
    w_fc1,
    fc1_bias,
    w_fc2,
    fc2_bias,
):
    shards = (
        ln1_gain[0],
        ln1_bias[0],
        w_qkv[0],
        qv_bias[0],
        w_out[0],
        out_bias[0],
        ln2_gain[0],
        ln2_bias[0],
        w_fc1[0],
        fc1_bias[0],
        w_fc2[0],
        fc2_bias[0],
    )
    gathered = (
        lax.all_gather(shards[0], "shard", axis=0, tiled=True),
        lax.all_gather(shards[1], "shard", axis=0, tiled=True),
        lax.all_gather(shards[2], "shard", axis=0, tiled=True),
        lax.all_gather(shards[3], "shard", axis=0, tiled=True),
        lax.all_gather(shards[4], "shard", axis=0, tiled=True),
        lax.all_gather(shards[5], "shard", axis=0, tiled=True),
        lax.all_gather(shards[6], "shard", axis=0, tiled=True),
        lax.all_gather(shards[7], "shard", axis=0, tiled=True),
        lax.all_gather(shards[8], "shard", axis=0, tiled=True),
        lax.all_gather(shards[9], "shard", axis=0, tiled=True),
        lax.all_gather(shards[10], "shard", axis=0, tiled=True),
        lax.all_gather(shards[11], "shard", axis=0, tiled=True),
    )
    weights = tuple(
        (member.astype(jnp.float32) if member.ndim == 1 else member for member in gathered)
    )
    section_zero = lax.axis_index("section") == 0
    local_data = boundary[0, :, 0].astype(jnp.float32)
    micro_count = local_data.shape[0]
    token_count = local_data.shape[1]
    start_row = lax.axis_index("shard") * token_count
    image_table = image_of_token[:, 0]
    empty_rows = jnp.zeros_like(local_data[0])
    stored_list = []
    resid_outs = []
    received = empty_rows
    for time_step in range(micro_count + 1):
        lower_input = local_data[time_step] if time_step < micro_count else empty_rows
        resid_in = jnp.where(section_zero, lower_input, received)
        image_ids = jnp.where(
            section_zero,
            image_table[min(time_step, micro_count - 1)],
            image_table[max(time_step - 1, 0)],
        )
        resid_out, stored = forward_block(weights, resid_in, image_ids, start_row)
        stored_list.append(stored)
        resid_outs.append(resid_out)
        if time_step < micro_count:
            received = from_behind(resid_out.astype(jnp.bfloat16), "section", 1).astype(jnp.float32)
    sent_back = empty_rows
    input_grads = []
    vector_sums = None
    pair_lists = [[], [], [], []]
    for time_step in range(micro_count + 1):
        lower_pick = time_step - 1 if time_step >= 1 else time_step + 1
        upper_pick = time_step + 1 if time_step < micro_count else time_step - 1
        stored = jax.tree.map(
            lambda lower_val, upper_val: jnp.where(section_zero, lower_val, upper_val),
            stored_list[lower_pick],
            stored_list[upper_pick],
        )
        upper_grad = local_data[time_step] if time_step < micro_count else empty_rows
        grad_out = jnp.where(section_zero, sent_back, upper_grad)
        d_resid, vectors, pair_terms = backward_block(weights, stored, grad_out, start_row)
        input_grads.append(d_resid)
        if vector_sums is None:
            vector_sums = vectors
        else:
            vector_sums = tuple((running + member for running, member in zip(vector_sums, vectors)))
        for pair_index in range(4):
            pair_lists[pair_index].append(pair_terms[pair_index])
        if time_step < micro_count:
            sent_back = from_behind(d_resid.astype(jnp.bfloat16), "section", -1).astype(jnp.float32)
    matrix_grads = []
    for pair_index in range(4):
        left_rows = jnp.concatenate(
            [entry_pair[0] for entry_pair in pair_lists[pair_index]], axis=0
        )
        right_rows = jnp.concatenate(
            [entry_pair[1] for entry_pair in pair_lists[pair_index]], axis=0
        )
        matrix_grads.append(over_rows(left_rows, right_rows))
    (
        d_ln1_gain,
        d_ln1_bias,
        d_qv_bias,
        d_out_bias,
        d_ln2_gain,
        d_ln2_bias,
        d_fc1_bias,
        d_fc2_bias,
    ) = vector_sums
    all_grads = (
        d_ln1_gain,
        d_ln1_bias,
        matrix_grads[0],
        d_qv_bias,
        matrix_grads[1],
        d_out_bias,
        d_ln2_gain,
        d_ln2_bias,
        matrix_grads[2],
        d_fc1_bias,
        matrix_grads[3],
        d_fc2_bias,
    )
    pieces = (
        lax.psum_scatter(all_grads[0], ("shard", "replica"), scatter_dimension=0, tiled=True),
        lax.psum_scatter(all_grads[1], ("shard", "replica"), scatter_dimension=0, tiled=True),
        lax.psum_scatter(all_grads[2], ("shard", "replica"), scatter_dimension=0, tiled=True),
        lax.psum_scatter(all_grads[3], ("shard", "replica"), scatter_dimension=0, tiled=True),
        lax.psum_scatter(all_grads[4], ("shard", "replica"), scatter_dimension=0, tiled=True),
        lax.psum_scatter(all_grads[5], ("shard", "replica"), scatter_dimension=0, tiled=True),
        lax.psum_scatter(all_grads[6], ("shard", "replica"), scatter_dimension=0, tiled=True),
        lax.psum_scatter(all_grads[7], ("shard", "replica"), scatter_dimension=0, tiled=True),
        lax.psum_scatter(all_grads[8], ("shard", "replica"), scatter_dimension=0, tiled=True),
        lax.psum_scatter(all_grads[9], ("shard", "replica"), scatter_dimension=0, tiled=True),
        lax.psum_scatter(all_grads[10], ("shard", "replica"), scatter_dimension=0, tiled=True),
        lax.psum_scatter(all_grads[11], ("shard", "replica"), scatter_dimension=0, tiled=True),
    )
    owner_part = (
        lax.all_gather(pieces[0].astype(jnp.bfloat16), "replica", axis=0, tiled=True).astype(
            jnp.float32
        ),
        lax.all_gather(pieces[1].astype(jnp.bfloat16), "replica", axis=0, tiled=True).astype(
            jnp.float32
        ),
        lax.all_gather(pieces[2].astype(jnp.bfloat16), "replica", axis=0, tiled=True).astype(
            jnp.float32
        ),
        lax.all_gather(pieces[3].astype(jnp.bfloat16), "replica", axis=0, tiled=True).astype(
            jnp.float32
        ),
        lax.all_gather(pieces[4].astype(jnp.bfloat16), "replica", axis=0, tiled=True).astype(
            jnp.float32
        ),
        lax.all_gather(pieces[5].astype(jnp.bfloat16), "replica", axis=0, tiled=True).astype(
            jnp.float32
        ),
        lax.all_gather(pieces[6].astype(jnp.bfloat16), "replica", axis=0, tiled=True).astype(
            jnp.float32
        ),
        lax.all_gather(pieces[7].astype(jnp.bfloat16), "replica", axis=0, tiled=True).astype(
            jnp.float32
        ),
        lax.all_gather(pieces[8].astype(jnp.bfloat16), "replica", axis=0, tiled=True).astype(
            jnp.float32
        ),
        lax.all_gather(pieces[9].astype(jnp.bfloat16), "replica", axis=0, tiled=True).astype(
            jnp.float32
        ),
        lax.all_gather(pieces[10].astype(jnp.bfloat16), "replica", axis=0, tiled=True).astype(
            jnp.float32
        ),
        lax.all_gather(pieces[11].astype(jnp.bfloat16), "replica", axis=0, tiled=True).astype(
            jnp.float32
        ),
    )
    stacked = jnp.stack(
        [
            jnp.where(section_zero, input_grads[micro_index + 1], resid_outs[micro_index + 1])
            for micro_index in range(micro_count)
        ]
    )
    boundary_out = stacked[None, :, None]
    return (boundary_out,) + tuple((member[None] for member in owner_part))


def solution(mesh):
    in_specs = (
        P("section", None, "replica", "shard", None),
        P(None, "replica", None),
        P("section", "shard"),
        P("section", "shard"),
        P("section", "shard", None),
        P("section", "shard"),
        P("section", "shard", None),
        P("section", "shard"),
        P("section", "shard"),
        P("section", "shard"),
        P("section", "shard", None),
        P("section", "shard"),
        P("section", "shard", None),
        P("section", "shard"),
    )
    out_specs = (
        P("section", None, "replica", "shard", None),
        P("section", "shard"),
        P("section", "shard"),
        P("section", "shard", None),
        P("section", "shard"),
        P("section", "shard", None),
        P("section", "shard"),
        P("section", "shard"),
        P("section", "shard"),
        P("section", "shard", None),
        P("section", "shard"),
        P("section", "shard", None),
        P("section", "shard"),
    )
    return jax.shard_map(body, mesh=mesh, in_specs=in_specs, out_specs=out_specs, check_vma=False)
```

profile of v0, /device:TPU:0, one launch (start us, length us, event | category | flops | bytes accessed | tf_op | source)
XLA Modules:
  0.0 2028.8 jit_solution(48523376486751329)
XLA Ops:
  8.0 10.8 all-gather
  28.0 9.5 all-gather.3
  38.5 14.6 all-gather.32.cloned.1.call-done
  95.1 11.5 all-gather.9
  122.6 41.9 %all-gather.36.cloned.1.call-done = bf16[1,1024,4096]{2,1,0:T(8,128)(2,1)} async-done(((bf16[1,128,4096]{2,1,0:T(8,128)(2,1)}), bf16[1,1024,4096]{2,1,0:T(8,128)(2,1)}) %all-gather.36.cloned.1.call-update) | async-done | bytes 8388624 | tf_op jit(solution)/shard_map/all_gather | solution.py:252
  173.8 42.3 %all-gather.38.cloned.1.call-done = bf16[1,4096,1024]{2,1,0:T(8,128)(2,1)} async-done(((bf16[1,512,1024]{2,1,0:T(8,128)(2,1)}), bf16[1,4096,1024]{2,1,0:T(8,128)(2,1)}) %all-gather.38.cloned.1.call-update) | async-done | bytes 8388624 | tf_op jit(solution)/shard_map/all_gather | solution.py:254
  234.2 28.0 %all-gather.24.cloned.1.call-done = bf16[768,2048]{1,0:T(8,128)(2,1)} async-done(((bf16[96,2048]{1,0:T(8,128)(2,1)}), bf16[768,2048]{1,0:T(8,128)(2,1)}) %all-gather.24.cloned.1.call-update) | async-done | bytes 3145744 | tf_op jit(solution)/shard_map/all_gather | solution.py:82
  323.4 29.0 %reduce-scatter.22.cloned.1.call-done = bf16[96,2048]{1,0:T(8,128)(2,1)} async-done(((bf16[768,2048]{1,0:T(8,128)(2,1)}), bf16[96,2048]{1,0:T(8,128)(2,1)}) %reduce-scatter.22.cloned.1.call-update) | async-done | bytes 393232
  380.5 11.7 all-gather.26.cloned.1.call-done
  461.9 28.5 %reduce-scatter.24.cloned.1.call-done = bf16[96,2048]{1,0:T(8,128)(2,1)} async-done(((bf16[768,2048]{1,0:T(8,128)(2,1)}), bf16[96,2048]{1,0:T(8,128)(2,1)}) %reduce-scatter.24.cloned.1.call-update) | async-done | bytes 393232
  545.1 11.7 fusion.84
  566.6 9.8 reduce-scatter.26.cloned.1.call-done
  577.7 9.8 fusion.72
  588.7 11.6 fusion.90
  613.5 283.8 %all-reduce.16 = (bf16[1024]{0:T(1024)(128)(2,1)S(1)}, bf16[1024]{0:T(1024)(128)(2,1)S(1)}, bf16[2048]{0:T(1024)(128)(2,1)S(1)}, bf16[1024]{0:T(1024)(128)(2,1)S...) all-reduce(f32[1024]{0:T(1024)S(1)} %add_add_fusion.15, ...), channel_id=17, replica_groups=mesh['section'=2,'shard'=8,'replica'=8] {'shard','replica'}, use_global_device_ids=true, to_apply=%region_43.44.clone | all-reduce | flops 12288 | bytes 73728
  899.7 17.9 all-reduce.17
  924.1 31.0 %reduce-scatter.18.cloned.1.call-done = f32[16,4096]{1,0:T(8,128)} async-done(((f32[1024,4096]{1,0:T(8,128)}), f32[16,4096]{1,0:T(8,128)}) %reduce-scatter.18.cloned.1.call-update) | async-done | bytes 262160 | tf_op jit(solution)/shard_map/reduce_scatter | solution.py:349
  960.9 291.3 %reduce-scatter.16.cloned.1.call-done = f32[16,1024]{1,0:T(8,128)} async-done(((f32[1024,1024]{1,0:T(8,128)}), f32[16,1024]{1,0:T(8,128)}) %reduce-scatter.16.cloned.1.call-update) | async-done | bytes 65552 | tf_op jit(solution)/shard_map/reduce_scatter | solution.py:345
  1253.0 31.9 %all_gather.100 = bf16[128,1024]{1,0:T(8,128)(2,1)S(1)} all-gather(bf16[16,1024]{1,0:T(8,128)(2,1)S(1)} %convert_element_type.334), channel_id=1, replica_groups=mesh['section'=2,'shard'=8,'replica'=8] {'replica'}, dimensions={0}, use_global_device_ids=true | all-gather | bytes 294912 | tf_op jit(solution)/shard_map/all_gather | solution.py:367
  1285.8 273.3 %reduce-scatter.14.cloned.1.call-done = f32[16,3072]{1,0:T(8,128)} async-done(((f32[1024,3072]{1,0:T(8,128)}), f32[16,3072]{1,0:T(8,128)}) %reduce-scatter.14.cloned.1.call-update) | async-done | bytes 196624 | tf_op jit(solution)/shard_map/reduce_scatter | solution.py:343
  1560.0 366.3 %reduce-scatter.20.cloned.1.call-done = f32[64,1024]{1,0:T(8,128)} async-done(((f32[4096,1024]{1,0:T(8,128)}), f32[64,1024]{1,0:T(8,128)}) %reduce-scatter.20.cloned.1.call-update) | async-done | bytes 262160 | tf_op jit(solution)/shard_map/reduce_scatter | solution.py:351
  1927.9 38.2 %all_gather.98 = bf16[128,3072]{1,0:T(8,128)(2,1)S(1)} all-gather(bf16[16,3072]{1,0:T(8,128)(2,1)S(1)} %convert_element_type.329), channel_id=1, replica_groups=mesh['section'=2,'shard'=8,'replica'=8] {'replica'}, dimensions={0}, use_global_device_ids=true | all-gather | bytes 884736 | tf_op jit(solution)/shard_map/all_gather | solution.py:361
  1967.4 9.9 all-gather.28.cloned.1.call-done
  1980.1 39.2 %all-gather.30.cloned.1.call-done = bf16[512,1024]{1,0:T(8,128)(2,1)} async-done(((bf16[64,1024]{1,0:T(8,128)(2,1)}), bf16[512,1024]{1,0:T(8,128)(2,1)}) %all-gather.30.cloned.1.call-update) | async-done | bytes 1048592 | tf_op jit(solution)/shard_map/all_gather | solution.py:385
  (653 shorter events, 354.5 us)
Async XLA Ops:
  7.2 45.9 %all-gather.32.cloned.1.call-start = ((), (), s32[]{:S(2)}) async-start(), calls=%async_computation.16 | async-start | bytes 7077888 | tf_op jit(solution)/shard_map/all_gather | solution.py:246
  7.9 99.7 %all-gather.22.cloned.1.call-start = ((), (), s32[]{:S(2)}) async-start(), calls=%async_computation.7 | async-start | bytes 3538944 | tf_op jit(solution)/shard_map/all_gather | solution.py:82
  58.0 62.1 %all-gather.34.cloned.1.call-start = ((), (), s32[]{:S(2)}) async-start(), calls=%async_computation.17 | async-start | bytes 2359296 | tf_op jit(solution)/shard_map/all_gather | solution.py:248
  58.8 105.8 %all-gather.36.cloned.1.call-start = ((), (), s32[]{:S(2)}) async-start(), calls=%async_computation.18 | async-start | bytes 9437184 | tf_op jit(solution)/shard_map/all_gather | solution.py:252
  59.4 156.7 %all-gather.38.cloned.1.call-start = ((), (), s32[]{:S(2)}) async-start(), calls=%async_computation.19 | async-start | bytes 9437184 | tf_op jit(solution)/shard_map/all_gather | solution.py:254
  59.9 202.2 %all-gather.24.cloned.1.call-start = ((), (), s32[]{:S(2)}) async-start(), calls=%async_computation.8 | async-start | bytes 3538944 | tf_op jit(solution)/shard_map/all_gather | solution.py:82
  221.1 9.5 collective-permute-start
  233.1 119.2 %reduce-scatter.22.cloned.1.call-start = ((), (), s32[]{:S(2)}) async-start(), calls=%async_computation.20 | async-start | bytes 3538944
  285.2 12.9 collective-permute-start.2
  318.9 73.4 %all-gather.26.cloned.1.call-start = ((), (), s32[]{:S(2)}) async-start(), calls=%async_computation.9 | async-start | bytes 3538944 | tf_op jit(solution)/shard_map/all_gather | solution.py:82
  365.5 125.0 %reduce-scatter.24.cloned.1.call-start = ((), (), s32[]{:S(2)}) async-start(), calls=%async_computation.21 | async-start | bytes 3538944
  369.9 9.3 collective-permute-start.1
  454.6 121.8 %reduce-scatter.26.cloned.1.call-start = ((), (), s32[]{:S(2)}) async-start(), calls=%async_computation.22 | async-start | bytes 3538944
  499.8 9.1 collective-permute-start.3
  542.9 412.3 %reduce-scatter.18.cloned.1.call-start = ((), (), s32[]{:S(2)}) async-start(), calls=%async_computation.12 | async-start | bytes 17039360 | tf_op jit(solution)/shard_map/reduce_scatter | solution.py:349
  556.8 695.3 %reduce-scatter.16.cloned.1.call-start = ((), (), s32[]{:S(2)}) async-start(), calls=%async_computation.11 | async-start | bytes 4259840 | tf_op jit(solution)/shard_map/reduce_scatter | solution.py:345
  561.6 997.5 %reduce-scatter.14.cloned.1.call-start = ((), (), s32[]{:S(2)}) async-start(), calls=%async_computation.10 | async-start | bytes 12779520 | tf_op jit(solution)/shard_map/reduce_scatter | solution.py:343
  587.6 1338.7 %reduce-scatter.20.cloned.1.call-start = ((), (), s32[]{:S(2)}) async-start(), calls=%async_computation.14 | async-start | bytes 17039360 | tf_op jit(solution)/shard_map/reduce_scatter | solution.py:351
  600.3 1377.1 %all-gather.28.cloned.1.call-start = ((), (), s32[]{:S(2)}) async-start(), calls=%async_computation.13 | async-start | bytes 1179648 | tf_op jit(solution)/shard_map/all_gather | solution.py:379
  608.3 310.8 %copy-start.40 = (bf16[96,4096]{1,0:T(8,128)(2,1)S(1)}, bf16[96,4096]{1,0:T(8,128)(2,1)}, u32[]{:S(2)}) copy-start(bf16[96,4096]{1,0:T(8,128)(2,1)} %get-tuple-element.95) | copy-start | bytes 2359300
  608.3 310.8 %copy-start.50 = (bf16[96,1024]{1,0:T(8,128)(2,1)S(1)}, bf16[96,1024]{1,0:T(8,128)(2,1)}, u32[]{:S(2)}) copy-start(bf16[96,1024]{1,0:T(8,128)(2,1)} %copy-done.49) | copy-start | bytes 589828
  608.3 310.8 %copy-start.90 = (f32[1,1024]{1,0:T(1,128)S(1)}, f32[1,1024]{1,0:T(1,128)}, u32[]{:S(2)}) copy-start(f32[1,1024]{1,0:T(1,128)} %copy-done.89) | copy-start | bytes 12292
  608.3 310.8 %copy-start.144 = (f32[96]{0:T(128)S(1)}, f32[96]{0:T(128)}, u32[]{:S(2)}) copy-start(f32[96]{0:T(128)} %copy-done.143) | copy-start | bytes 1156
  956.8 1062.5 %all-gather.30.cloned.1.call-start = ((), (), s32[]{:S(2)}) async-start(), calls=%async_computation.15 | async-start | bytes 1179648 | tf_op jit(solution)/shard_map/all_gather | solution.py:385
  (183 other events, 3790.2 us)
Sparse Core Ops, SparseCore 0:
  9.7 43.3 all-gather.31
  58.2 27.8 all-gather.21
  87.7 25.1 all-gather.33
  114.5 50.0 all-gather.35
  166.1 49.8 all-gather.37
  233.3 28.8 all-gather.23
  319.0 33.2 reduce-scatter.21
  365.6 26.5 all-gather.25
  454.7 35.7 reduce-scatter.23
  543.0 33.3 reduce-scatter.25
  578.8 376.3 reduce-scatter.17
  957.4 294.7 reduce-scatter.15
  1254.7 304.2 reduce-scatter.13
  1561.4 364.7 reduce-scatter.19
  1928.4 48.8 all-gather.27
  1978.9 40.2 all-gather.29
where the time goes:
time: 2030 us
  waiting for transfers between devices  1240 us (61%)
  blocking collectives  447 us (22%)
  matrix products  170 us (8%)
  local copies, waits for them, and re-layouts  81 us (4%)
  other arithmetic  58.5 us (3%)
  between operations  20.6 us (1%)
    reduce_scatter x1, waiting for transfers between devices, body(): lax.psum_scatter(all_grads[10], ('shard', 'replica'), scatter_dimension=0...  366 us
    unnamed x2, blocking collectives  302 us
    reduce_scatter x1, waiting for transfers between devices, body(): lax.psum_scatter(all_grads[4], ('shard', 'replica'), scatter_dimension=0,...  291 us
    reduce_scatter x1, waiting for transfers between devices, body(): lax.psum_scatter(all_grads[2], ('shard', 'replica'), scatter_dimension=0,...  273 us
    unnamed x19, waiting for transfers between devices  69.9 us
    dot_general x12, matrix products, matmul_t(): lax.dot_general(first_op, second_op, (((1,), (1,)), ((), ())), preferred_...  48.2 us
    all_gather x1, waiting for transfers between devices, body(): lax.all_gather(shards[10], 'shard', axis=0, tiled=True)  42.3 us
    dot_general x12, matrix products, matmul(): return jnp.dot(first_op, second_op, preferred_element_type=jnp.float32)  42.2 us
  transfers between devices with their start and end apart: 20, of which 17 were waited for; matrix products, arithmetic and copies ran while one was open for 6% of the time, Pallas kernels for 0%

commit v1 on v0

v1 whole, which is shorter than its diff:
```python
import functools

import jax
import jax.numpy as jnp
from jax import lax
from jax.experimental import pallas as pl
from jax.experimental.pallas import tpu as pltpu
from jax.sharding import PartitionSpec as P

D = 1024
HEADS = 16
HEAD = 64
FF = 4096
EPS = 1e-06
NEG = -1e30

MICRO = 2
CHIPS = 4
ROWS = 96
TOK = CHIPS * ROWS
KEYS = 2 * TOK
WQ = 3 * D // CHIPS
WO = D // CHIPS
W1 = FF // CHIPS
REPL = 8

MESH = pl.DeviceIdType.MESH
F32 = jnp.float32
BF16 = jnp.bfloat16

AG1, RS1, AG2, RS2, BAG1, BRS1, BAG2, BRS2 = range(8)


def mm(a, b):
    return jnp.dot(a, b, preferred_element_type=F32)


def mm_t(a, b):
    return lax.dot_general(a, b, (((1,), (1,)), ((), ())), preferred_element_type=F32)


def over_rows(a, b):
    return lax.dot_general(a, b, (((0,), (0,)), ((), ())), preferred_element_type=F32)


def norm_parts(v):
    centered = v - jnp.mean(v, axis=-1, keepdims=True)
    rstd = lax.rsqrt(jnp.mean(centered * centered, axis=-1, keepdims=True) + EPS)
    return centered * rstd, rstd


def gray(k):
    return k + k // 2 - 2 * (k // 3)


def flip(r):
    return r + 1 - 2 * lax.rem(r, 2)


def copy_to(src, dst, send, recv, where):
    return pltpu.make_async_remote_copy(
        src_ref=src, dst_ref=dst, send_sem=send, recv_sem=recv, device_id=where, device_id_type=MESH
    )


QKV = {1: 0, 5: 1, 6: 2}


def piece_kinds():
    table = {kind: (0, 1, 3, 2) for kind in (0, 1, 2, 5, 6)}
    table.update({3: (0,), 4: (0,)})
    return table


def step_kernel(
    bnd, idr, v_ln1g, v_ln1b, v_qv, v_out, v_ln2g, v_ln2b, v_fc1, v_fc2, wq_s, wo_s, w1_s, w2_s,
    edge_o, fv, f1, fa, fc, f2,
    idc, vec_s, vecs, wq, wo, w1, w2,
    n1, n2, act, dgl, qkv, kvp, wt, rin, rmid, g, ga, dh, dp, dw,
    stage, landed, swap, carry_s, carry_r, dkv, dkv_s, dkv_r, own, gnext,
    pga, pgb, pgc, pgd, rga, rgb, rgc, rgd, lga, lgb, lgc, lgd,
    vg_o, em, ea, ec, zm, za, zc, ym, ya, yc, pm, p2, pa, pc, q1, qt, qa, lv, tv, zv, yv,
    xs_sem, xr_sem, ks_sem, kr_sem, ds_sem, dr_sem, cs_sem, cr_sem,
    wxs, wxr, wns, wnr, was, war, wfs, wfr, loc_sem, ps_sem, pr_sem, rs_sem, rr_sem, out_sem,
    zs_sem, zr_sem, as_sem, ar_sem, hs_sem, hr_sem, ys_sem, yr_sem, vs_sem, vr_sem, us_sem, ur_sem,
):
    sec = lax.axis_index("section")
    me = lax.axis_index("shard")
    rep = lax.axis_index("replica")
    x = me // 2
    c = me % 2
    mate = {"shard": x * 2 + 1 - c}
    other = {"section": 1 - sec}
    across_to = {"section": 1 - sec, "replica": flip(rep)}
    kinds = piece_kinds()

    def peer(d):
        return lax.rem(x + d, CHIPS)

    def at_peer(d):
        return {"shard": peer(d) * 2 + c}

    def at_rep(j):
        return {"replica": lax.rem(rep + j, REPL)}

    def at_shard(j):
        return {"shard": lax.rem(me + j, 8)}

    barrier = pltpu.get_barrier_semaphore()
    for j in range(1, REPL):
        pl.semaphore_signal(barrier, inc=1, device_id=at_shard(j), device_id_type=MESH)
        pl.semaphore_signal(barrier, inc=1, device_id=at_rep(j), device_id_type=MESH)
    for where in (other, across_to):
        pl.semaphore_signal(barrier, inc=1, device_id=where, device_id_type=MESH)
    pl.semaphore_wait(barrier, 16)

    def rows_of(chip):
        return pl.ds(pl.multiple_of(chip * ROWS, 32), ROWS)

    def w_src(kind, chip):
        if kind == 0:
            return vec_s
        if kind in (1, 5, 6):
            return wq_s.at[:, pl.ds(pl.multiple_of(QKV[kind] * D + chip * WO, WO), WO)]
        if kind == 2:
            return w1_s.at[:, pl.ds(pl.multiple_of(chip * W1, W1), W1)]
        return wo_s if kind == 3 else w2_s

    def w_dst(layer, kind, chip, core):
        if kind == 0:
            return vecs.at[layer, chip * 2 + core]
        if kind in (1, 2, 5, 6):
            rows = pl.ds(pl.multiple_of((chip * 2 + core) * 128, 128), 128)
            if kind == 2:
                return w1.at[layer, rows]
            return wq.at[layer, rows, pl.ds(QKV[kind] * WO, WO)]
        if kind == 3:
            return wo.at[layer, pl.ds(pl.multiple_of(core * 128, 128), 128)]
        return w2.at[layer, pl.ds(pl.multiple_of(core * 512, 512), 512)]

    def x_copy(kind, d, owner):
        return copy_to(
            w_src(kind, peer(d)), w_dst(sec, kind, owner, c), wxs.at[kind, d], wxr.at[kind, d], at_peer(d)
        )

    def own_piece(kind, d):
        return w_src(kind, x) if d == 0 else w_dst(sec, kind, peer(4 - d), c)

    def near_copy(kind, d, core):
        dst = w_dst(sec, kind, peer(4 - d), core)
        return copy_to(own_piece(kind, d), dst, wns.at[kind, d], wnr.at[kind, d], mate)

    def across_copy(kind, d, layer):
        dst = w_dst(layer, kind, peer(4 - d), c)
        return copy_to(own_piece(kind, d), dst, was.at[kind, d], war.at[kind, d], across_to)

    def far_copy(kind, d, core):
        ref = w_dst(1 - sec, kind, peer(4 - d), core)
        return copy_to(ref, ref, wfs.at[kind, d], wfr.at[kind, d], mate)

    def local_copy(kind):
        return pltpu.make_async_copy(w_src(kind, x), w_dst(sec, kind, x, c), loc_sem.at[kind])

    def launch(kind):
        if kind not in (3, 4):
            for d in (1, 3, 2):
                x_copy(kind, d, x).start()
        near_copy(kind, 0, c).start()
        local_copy(kind).start()

    def settle_near(kind):
        across_copy(kind, 0, sec).start()
        for d in kinds[kind][1:]:
            x_copy(kind, d, peer(4 - d)).wait_recv()
            near_copy(kind, d, c).start()
            across_copy(kind, d, sec).start()
        local_copy(kind).wait()
        for d in kinds[kind]:
            near_copy(kind, d, 1 - c).wait_recv()

    def settle_far(kind):
        for d in kinds[kind]:
            across_copy(kind, d, 1 - sec).wait_recv()
            far_copy(kind, d, c).start()
        for d in kinds[kind]:
            far_copy(kind, d, 1 - c).wait_recv()

    swap_copy = copy_to(bnd.at[1 - sec], swap, cs_sem.at[0], cr_sem.at[0], other)
    carry_copy = copy_to(carry_s, carry_r, cs_sem.at[1], cr_sem.at[1], other)

    at = 0
    for v in (v_ln1g, v_ln1b, v_qv, v_out, v_ln2g, v_ln2b, v_fc1, v_fc2):
        for t in range(v.shape[1] // 128):
            vec_s[at : at + 1, :] = v[:, t * 128 : t * 128 + 128].astype(F32)
            at += 1
    launch(0)
    swap_copy.start()
    for kind in QKV:
        launch(kind)
    idc[...] = jnp.transpose(jnp.broadcast_to(idr[:1, :], (128, KEYS)))
    settle_near(0)
    settle_far(0)
    swap_copy.wait_recv()

    @pl.when(sec == 0)
    def _():
        rin[0] = bnd[0].astype(F32)
        gnext[...] = swap[...].astype(F32)

    @pl.when(sec == 1)
    def _():
        rin[0] = swap[...].astype(F32)
        gnext[...] = bnd[1].astype(F32)

    def vec_row(l, k):
        return jnp.concatenate([vecs[l, i, k : k + 1, :] for i in range(8)], axis=1)

    def pieces(l, i, ks):
        part = vecs[l, i]
        return [part[k : k + 1, :] for k in ks]

    def gather_copy(buf, kind, l, d, owner):
        ref = buf.at[l, rows_of(owner)]
        return copy_to(ref, ref, xs_sem.at[kind, l, d], xr_sem.at[kind, l, d], at_peer(d))

    def scatter_copy(kind, l, d):
        return copy_to(
            stage.at[d - 1],
            landed.at[kind // 2, d - 1],
            xs_sem.at[kind, l, d],
            xr_sem.at[kind, l, d],
            at_peer(d),
        )

    def gather_start(buf, kind, l):
        for d in (1, 3, 2):
            gather_copy(buf, kind, l, d, x).start()

    def gather_wait(buf, kind, l, d):
        gather_copy(buf, kind, l, d, peer(4 - d)).wait_recv()

    def scatter_add(kind, l, base):
        total = base
        for d in (1, 3, 2):
            scatter_copy(kind, l, d).wait_recv()
            total = total + landed[kind // 2, d - 1].astype(F32)
        for d in (1, 3, 2):
            scatter_copy(kind, l, d).wait_send()
        return total

    def send_part(kind, l, d, part):
        @pl.when(d == 0)
        def _():
            own[...] = part

        @pl.when(d != 0)
        def _():
            stage[d - 1] = part.astype(BF16)
            scatter_copy(kind, l, d).start()

    def kv_copy(l, d):
        rows = rows_of(peer(4 - d))
        return copy_to(
            qkv.at[l, rows, pl.ds(WO, 2 * WO)], kvp.at[l, rows], ks_sem.at[l, d], kr_sem.at[l, d], mate
        )

    lane = lax.broadcasted_iota(jnp.int32, (1, 128), 1)

    def forward(l, first):
        need_far = l + sec == 1
        qkv_b = jnp.concatenate(
            pieces(l, x, (2, 3)) + [jnp.zeros((1, WO), F32)] + pieces(l, 4 + x, (2, 3)), axis=1
        )
        fc1_b = jnp.concatenate(
            pieces(l, 2 * x, (7, 8, 9, 10)) + pieces(l, 2 * x + 1, (7, 8, 9, 10)), axis=1
        )
        normed, _ = norm_parts(rin[l])
        n1[l, rows_of(x)] = (normed * vec_row(l, 0) + vec_row(l, 1)).astype(BF16)
        gather_start(n1, AG1, l)

        @pl.when(l == 0)
        def _():
            for kind in QKV:
                settle_near(kind)
            launch(3)
            launch(2)
            launch(4)

        @pl.when(need_far)
        def _():
            for kind in QKV:
                settle_far(kind)

        def project(k, _):
            d = gray(k)
            rows = rows_of(peer(4 - d))

            @pl.when(d != 0)
            def _():
                gather_wait(n1, AG1, l, d)

            qkv[l, rows] = (mm(n1[l, rows], wq[l]) + qkv_b).astype(BF16)
            kv_copy(l, d).start()
            return 0

        lax.fori_loop(0, CHIPS, project, 0)

        @pl.when(l == 0)
        def _():
            settle_near(3)
            settle_near(2)

        @pl.when(need_far)
        def _():
            settle_far(3)

        for d in range(CHIPS):
            kv_copy(l, d).wait_recv()

        def attend(j, _):
            d = gray(lax.rem(j + 1, CHIPS))
            rows = rows_of(peer(d))
            bias = jnp.where(idc[rows][:, :1] == idr[:1, :], 0.0, NEG)
            for pair in range(2):
                lanes = slice(pair * 128, pair * 128 + 128)
                q = qkv[l, rows, lanes] * jnp.asarray(HEAD**-0.5, BF16)
                k_own = qkv[l, :, WO + pair * 128 : WO + pair * 128 + 128]
                v_own = qkv[l, :, 2 * WO + pair * 128 : 2 * WO + pair * 128 + 128]
                k_par = kvp[l, :, lanes]
                v_par = kvp[l, :, WO + pair * 128 : WO + pair * 128 + 128]
                outs = []
                for half in range(2):
                    qm = jnp.where(lane // HEAD == half, q, jnp.zeros_like(q))
                    s = jnp.concatenate([mm_t(qm, k_own), mm_t(qm, k_par)], axis=1) + bias
                    p = jnp.exp(s - jnp.max(s, axis=1, keepdims=True))
                    p = (p / jnp.sum(p, axis=1, keepdims=True)).astype(BF16)
                    outs.append(mm(p[:, :TOK], v_own) + mm(p[:, TOK:], v_par))
                wt[l, rows, lanes] = jnp.where(lane < HEAD, outs[0], outs[1]).astype(BF16)
            send_part(RS1, l, d, mm(wt[l, rows], wo[l]))
            return 0

        lax.fori_loop(0, CHIPS, attend, 0)
        rmid[l] = rin[l] + (scatter_add(RS1, l, own[...]) + vec_row(l, 4))
        normed, _ = norm_parts(rmid[l])
        n2[l, rows_of(x)] = (normed * vec_row(l, 5) + vec_row(l, 6)).astype(BF16)
        gather_start(n2, AG2, l)

        @pl.when(l == 0)
        def _():
            settle_near(4)

        @pl.when(need_far)
        def _():
            settle_far(2)
            settle_far(4)

        def feed(k, _):
            d = gray(k)
            back = lax.rem(4 - d, CHIPS)
            rows = rows_of(peer(back))

            @pl.when(d != 0)
            def _():
                gather_wait(n2, AG2, l, d)

            h = mm(n2[l, rows], w1[l]) + fc1_b
            phi = 0.5 + 0.5 * lax.erf(h * (0.5**0.5))
            act[l, rows] = (h * phi).astype(BF16)
            dgl[l, rows] = phi + h * (jnp.exp(-0.5 * h * h) * 0.3989422804014327)
            send_part(RS2, l, back, mm(act[l, rows], w2[l]))
            return 0

        lax.fori_loop(0, CHIPS, feed, 0)
        out = rmid[l] + (scatter_add(RS2, l, own[...]) + vec_row(l, 11))

        @pl.when(l == 0)
        def _():
            rin[1] = out.astype(BF16).astype(F32)

        @pl.when((l == 1) & (sec == 0))
        def _():
            carry_s[...] = out.astype(BF16)
            carry_copy.start()

        @pl.when((l == 1) & (sec == 1))
        def _():
            edge_o[1] = out

        return first

    lax.fori_loop(0, 2, forward, 0)

    vg_o[...] = jnp.zeros_like(vg_o)

    def col_sum(v):
        return jnp.sum(v, axis=0, keepdims=True)

    def dkv_copy(l):
        return copy_to(dkv_s.at[l], dkv_r.at[l], ds_sem.at[l], dr_sem.at[l], mate)

    def grads_mlp(l):
        def block(t, _):
            cols = pl.ds(pl.multiple_of(t * 256, 256), 256)
            pgb[t] = over_rows(n2[l, :, cols], dh[l]).astype(BF16).reshape(2, 128, W1)
            half = pl.ds(pl.multiple_of(lax.rem(t, 2) * 256, 256), 256)
            pgd[t // 2, half] = over_rows(act[l, :, cols], g[l]).astype(BF16)
            return 0

        lax.fori_loop(0, CHIPS, block, 0)

    def grads_att(l):
        def block(t, _):
            cols = pl.ds(pl.multiple_of(t * 256, 256), 256)
            pga[t] = over_rows(n1[l, :, cols], dp[l]).astype(BF16).reshape(2, 128, WQ)
            return 0

        lax.fori_loop(0, CHIPS, block, 0)
        pgc[...] = over_rows(wt[l], ga[l]).astype(BF16).reshape(2, 128, D)

    def pair_mlp(l):
        return (
            copy_to(pgb.at[:, 1 - c], rgb, ps_sem.at[l, 1], pr_sem.at[l, 1], mate),
            copy_to(pgd.at[1 - c], rgd, ps_sem.at[l, 3], pr_sem.at[l, 3], mate),
        )

    def pair_att(l):
        return (
            copy_to(pga.at[:, 1 - c], rga, ps_sem.at[l, 0], pr_sem.at[l, 0], mate),
            copy_to(pgc.at[1 - c], rgc, ps_sem.at[l, 2], pr_sem.at[l, 2], mate),
        )

    def piece_of(l, r):
        return r + (l + sec - 2 * l * sec) * (1 - 2 * lax.rem(r, 2))

    def few(p):
        return pl.ds(pl.multiple_of(p * 16, 16), 16)

    def more(p):
        return pl.ds(pl.multiple_of(p * 64, 64), 64)

    def spread_copy(l, n, j):
        p = piece_of(l, lax.rem(rep + j, REPL))
        src = (rga.at[:, few(p)], rgb.at[:, few(p)], rgc.at[few(p)], rgd.at[more(p)])[n]
        return copy_to(src, (lga, lgb, lgc, lgd)[n].at[l, j], rs_sem.at[l, n, j], rr_sem.at[l, n, j], at_rep(j))

    def each_piece(l, ns, act_on):
        def one(j, _):
            for n in ns:
                act_on(spread_copy(l, n, j))
            return 0

        lax.fori_loop(1, REPL, one, 0)

    def sent(cp):
        cp.wait_send()

    def arrived(cp):
        cp.wait_recv()

    def begin(cp):
        cp.start()

    def both(u, v):
        return (u.astype(F32) + v.astype(F32)).astype(BF16)

    def spread_mlp(l):
        for cp in pair_mlp(l):
            cp.wait_recv()
        for t in range(CHIPS):
            rgb[t] = both(pgb[t, c], rgb[t])
        rgd[...] = both(pgd[c], rgd[...])
        p = piece_of(l, rep)
        for t in range(CHIPS):
            em[l, t * 16 : t * 16 + 16] = rgb[t, few(p)].astype(F32)
        em[l, 64:] = rgd[more(p)].astype(F32)
        each_piece(l, (1, 3), begin)

    def spread_att(l):
        for cp in pair_att(l):
            cp.wait_recv()
        for t in range(CHIPS):
            rga[t] = both(pga[t, c], rga[t])
        rgc[...] = both(pgc[c], rgc[...])
        p = piece_of(l, rep)
        for t in range(CHIPS):
            ea[l, t * 16 : t * 16 + 16] = rga[t, few(p)].astype(F32)
        ec[l] = rgc[few(p)].astype(F32)
        each_piece(l, (0, 2), begin)

    def collect_mlp(l):
        each_piece(l, (1, 3), arrived)
        for t in range(CHIPS):
            rows = slice(t * 16, t * 16 + 16)
            total = em[l, rows]
            for j in range(1, REPL):
                total = total + lgb[l, j, t].astype(F32)
            em[l, rows] = total
        total = em[l, 64:]
        for j in range(1, REPL):
            total = total + lgd[l, j].astype(F32)
        em[l, 64:] = total

    def collect_att(l):
        each_piece(l, (0, 2), arrived)
        for t in range(CHIPS):
            rows = slice(t * 16, t * 16 + 16)
            total = ea[l, rows]
            for j in range(1, REPL):
                total = total + lga[l, j, t].astype(F32)
            ea[l, rows] = total
        total = ec[l]
        for j in range(1, REPL):
            total = total + lgc[l, j].astype(F32)
        ec[l] = total

    def backward(i, first):
        l = 1 - i

        def add_vec(k, v):
            vg_o[l, k : k + 1, : v.shape[1]] += v

        def norm_back(v, gain, dy, k):
            xhat, rstd = norm_parts(v)
            add_vec(k, col_sum(dy * xhat))
            add_vec(k + 1, col_sum(dy))
            dyg = dy * gain
            return rstd * (
                dyg - jnp.mean(dyg, axis=-1, keepdims=True) - xhat * jnp.mean(dyg * xhat, axis=-1, keepdims=True)
            )

        low = gnext[...].astype(BF16)
        g[l, rows_of(x)] = low
        gather_start(g, BAG1, l)
        add_vec(7, col_sum(low.astype(F32)))

        @pl.when(i == 1)
        def _():
            grads_att(1)
            each_piece(1, (1, 3), sent)
            for cp in pair_att(1):
                cp.start()
            collect_mlp(1)

        def feed(k, _):
            d = gray(k)
            back = lax.rem(4 - d, CHIPS)
            rows = rows_of(peer(back))

            @pl.when(d != 0)
            def _():
                gather_wait(g, BAG1, l, d)

            d_low = (mm_t(g[l, rows], w2[l]) * dgl[l, rows]).astype(BF16)
            dh[l, rows] = d_low
            add_vec(6, col_sum(d_low.astype(F32)))
            send_part(BRS1, l, back, mm_t(d_low, w1[l]))
            return 0

        lax.fori_loop(0, CHIPS, feed, 0)

        @pl.when(i == 1)
        def _():
            spread_att(1)
            for cp in pair_mlp(1):
                cp.wait_send()

        grads_mlp(l)
        for cp in pair_mlp(l):
            cp.start()
        dn2 = scatter_add(BRS1, l, own[...])
        d_mid = gnext[...] + norm_back(rmid[l], vec_row(l, 5), dn2, 4)
        rmid[l] = d_mid
        low = d_mid.astype(BF16)
        ga[l, rows_of(x)] = low
        gather_start(ga, BAG2, l)
        add_vec(3, col_sum(low.astype(F32)))

        def expand(k, _):
            d = gray(k)
            rows = rows_of(peer(4 - d))

            @pl.when(d != 0)
            def _():
                gather_wait(ga, BAG2, l, d)

            dw[rows] = mm_t(ga[l, rows], wo[l]).astype(BF16)
            return 0

        lax.fori_loop(0, CHIPS, expand, 0)
        spread_mlp(l)
        dkv[...] = jnp.zeros_like(dkv)

        def attend(b, _):
            rows = pl.ds(pl.multiple_of(b * 128, 128), 128)
            bias = jnp.where(idc[:, :1] == idr[:, rows][:1, :], 0.0, NEG)
            for pair in range(2):
                lanes = slice(pair * 128, pair * 128 + 128)
                q = qkv[l, rows, lanes] * jnp.asarray(HEAD**-0.5, BF16)
                do = dw[rows, lanes]
                k_all = jnp.concatenate(
                    [qkv[l, :, WO + pair * 128 : WO + pair * 128 + 128], kvp[l, :, lanes]], axis=0
                )
                v_all = jnp.concatenate(
                    [
                        qkv[l, :, 2 * WO + pair * 128 : 2 * WO + pair * 128 + 128],
                        kvp[l, :, WO + pair * 128 : WO + pair * 128 + 128],
                    ],
                    axis=0,
                )
                dqs = []
                for half in range(2):
                    keep = lane // HEAD == half
                    qm = jnp.where(keep, q, jnp.zeros_like(q))
                    dom = jnp.where(keep, do, jnp.zeros_like(do))
                    s = mm_t(k_all, qm) + bias
                    p = jnp.exp(s - jnp.max(s, axis=0, keepdims=True))
                    p = p * (1.0 / jnp.sum(p, axis=0, keepdims=True))
                    dpr = mm_t(v_all, dom)
                    ds = (p * (dpr - jnp.sum(p * dpr, axis=0, keepdims=True))).astype(BF16)
                    dkv[:, lanes] += mm(ds, qm)
                    dkv[:, WO + pair * 128 : WO + pair * 128 + 128] += mm(p.astype(BF16), dom)
                    dqs.append(over_rows(ds, k_all))
                dq = jnp.where(lane < HEAD, dqs[0], dqs[1]) * (HEAD**-0.5)
                dp[l, rows, lanes] = dq.astype(BF16)
            return 0

        lax.fori_loop(0, TOK // 128, attend, 0)
        dkv_s[l] = dkv[TOK:].astype(BF16)

        @pl.when(i == 1)
        def _():
            collect_att(1)
            each_piece(1, (0, 2), sent)

        dkv_copy(l).start()
        dkv_copy(l).wait_recv()
        dp[l, :, WO:] = (dkv[:TOK] + dkv_r[l].astype(F32)).astype(BF16)
        add_vec(
            2,
            jnp.concatenate(
                [col_sum(dp[l, :, :WO].astype(F32)), col_sum(dp[l, :, 2 * WO :].astype(F32))], axis=1
            ),
        )

        @pl.when(i == 1)
        def _():
            for cp in pair_att(1):
                cp.wait_send()
            grads_att(0)
            for cp in pair_att(0):
                cp.start()

        def shrink(j, _):
            d = gray(lax.rem(j + 1, CHIPS))
            send_part(BRS2, l, d, mm_t(dp[l, rows_of(peer(d))], wq[l]))
            return 0

        lax.fori_loop(0, CHIPS, shrink, 0)

        @pl.when(i == 1)
        def _():
            spread_att(0)

        dn1 = scatter_add(BRS2, l, own[...])
        d_in = rmid[l] + norm_back(rin[l], vec_row(l, 0), dn1, 0)

        @pl.when(i == 0)
        def _():
            gnext[...] = d_in.astype(BF16).astype(F32)

        @pl.when((i == 1) & (sec == 1))
        def _():
            carry_s[...] = d_in.astype(BF16)
            carry_copy.start()

        @pl.when((i == 1) & (sec == 0))
        def _():
            edge_o[0] = d_in

        return first

    lax.fori_loop(0, 2, backward, 0)

    def vec_copy(j):
        return copy_to(vg_o, lv.at[j], vs_sem.at[j], vr_sem.at[j], at_rep(j))

    def vec_share(j, slot):
        return copy_to(tv, fv.at[slot], us_sem.at[j], ur_sem.at[j], at_shard(j))

    def cross_copy(n):
        src, dst = ((zm, ym), (za, ya), (zc, yc), (zv, yv))[n]
        return copy_to(src, dst, zs_sem.at[n], zr_sem.at[n], across_to)

    def turn_refs(n, source):
        if n == 0:
            return pm, q1.at[:, pl.ds(pl.multiple_of(source * W1, W1), W1)]
        return pa, qt.at[few(source)]

    def turn_copy(n, d, source):
        src, dst = turn_refs(n, source)
        return copy_to(src.at[few(peer(d))], dst, as_sem.at[n, d], ar_sem.at[n, d], at_peer(d))

    def turn_start(n):
        for d in (1, 3, 2):
            turn_copy(n, d, x).start()
        src, dst = turn_refs(n, x)
        dst[...] = src[few(x)]

    def turn_wait(n):
        for d in (1, 3, 2):
            turn_copy(n, d, peer(4 - d)).wait_recv()

    zi = rep // 2
    yi = lax.rem(rep, 2)
    y_mate = {"replica": flip(rep)}
    pieces_of = ((q1, f1), (qa, fa), (pc, fc), (p2, f2))

    def slot_ref(n, slot):
        return pieces_of[n][1].at[more(slot) if n == 3 else few(slot)]

    def slot_of(d, y):
        return lax.rem(zi + 4 - d, 4) * 2 + y

    def along_z(n, d, slot):
        src = pieces_of[n][0]
        where = {"replica": lax.rem(zi + d, 4) * 2 + yi}
        return copy_to(src, slot_ref(n, slot), hs_sem.at[n, d], hr_sem.at[n, d], where)

    def along_y(n, d, y):
        dst = slot_ref(n, slot_of(d, y))
        return copy_to(pieces_of[n][0] if d == 0 else dst, dst, ys_sem.at[n, d], yr_sem.at[n, d], y_mate)

    def keep_piece(n):
        return pltpu.make_async_copy(pieces_of[n][0], slot_ref(n, rep), out_sem.at[n])

    def share_start(n):
        along_y(n, 0, yi).start()
        for d in (1, 3, 2):
            along_z(n, d, rep).start()
        keep_piece(n).start()

    def share_on(n):
        for d in (1, 3, 2):
            along_z(n, d, slot_of(d, yi)).wait_recv()
            along_y(n, d, yi).start()

    for j in range(1, REPL):
        vec_copy(j).start()
    collect_mlp(0)
    zm[...] = em[1 - sec].astype(BF16)
    cross_copy(0).start()
    total = vg_o[...]
    for j in range(1, REPL):
        vec_copy(j).wait_recv()
        total = total + lv[j]
    vg_o_sum = total
    zv[...] = jnp.where(sec == 0, vg_o_sum[1], vg_o_sum[0])
    cross_copy(3).start()
    cross_copy(0).wait_recv()
    pm[...] = (em[sec, :64] + ym[:64].astype(F32)).astype(BF16)
    p2[...] = (em[sec, 64:] + ym[64:].astype(F32)).astype(BF16)
    turn_start(0)
    share_start(3)
    turn_wait(0)
    share_start(0)
    collect_att(0)
    za[...] = ea[1 - sec].astype(BF16)
    zc[...] = ec[1 - sec].astype(BF16)
    cross_copy(1).start()
    cross_copy(2).start()
    cross_copy(3).wait_recv()
    tv[...] = jnp.where(sec == 0, vg_o_sum[0], vg_o_sum[1]) + yv[...]
    fv[me] = tv[...]
    for j in range(1, REPL):
        vec_share(j, me).start()
    cross_copy(1).wait_recv()
    cross_copy(2).wait_recv()
    pa[...] = (ea[sec] + ya[...].astype(F32)).astype(BF16)
    pc[...] = (ec[sec] + yc[...].astype(F32)).astype(BF16)
    turn_start(1)
    share_start(2)
    turn_wait(1)
    for t in range(3):
        for chip in range(CHIPS):
            at = t * D + chip * WO
            qa[:, at : at + WO] = qt[chip * 16 : chip * 16 + 16, t * WO : t * WO + WO]
    share_start(1)
    share_on(3)
    share_on(0)
    share_on(2)
    share_on(1)
    for n in range(4):
        for d in range(4):
            along_y(n, d, 1 - yi).wait_recv()
        keep_piece(n).wait()
    for j in range(1, REPL):
        vec_share(j, lax.rem(me + 8 - j, 8)).wait_recv()

    carry_copy.wait_recv()
    edge_o[1 - sec] = carry_r[...].astype(F32)
    carry_copy.wait_send()
    swap_copy.wait_send()
    for kind in kinds:
        for d in kinds[kind]:
            if d != 0:
                x_copy(kind, d, x).wait_send()
            near_copy(kind, d, c).wait_send()
            across_copy(kind, d, sec).wait_send()
            far_copy(kind, d, c).wait_send()
    for l in range(2):
        for d in (1, 2, 3):
            for buf, kind in ((n1, AG1), (n2, AG2), (g, BAG1), (ga, BAG2)):
                gather_copy(buf, kind, l, d, x).wait_send()
        for d in range(CHIPS):
            kv_copy(l, d).wait_send()
        dkv_copy(l).wait_send()
    each_piece(0, (0, 1, 2, 3), sent)
    for cp in pair_mlp(0) + pair_att(0):
        cp.wait_send()
    for n in range(4):
        cross_copy(n).wait_send()
    for n in range(2):
        for d in (1, 2, 3):
            turn_copy(n, d, x).wait_send()
    for n in range(4):
        for d in (1, 2, 3):
            along_z(n, d, rep).wait_send()
        for d in range(4):
            along_y(n, d, yi).wait_send()
    for j in range(1, REPL):
        vec_copy(j).wait_send()
        vec_share(j, me).wait_send()


def run_step(*operands):
    vm = pl.BlockSpec(memory_space=pltpu.VMEM)
    hbm = pl.BlockSpec(memory_space=pl.ANY)
    sds = jax.ShapeDtypeStruct
    dma = pltpu.SemaphoreType.DMA
    return pl.pallas_call(
        step_kernel,
        out_shape=(
            sds((MICRO, ROWS, D), F32),
            sds((8, 8, D), F32),
            sds((128, FF), BF16),
            sds((128, 3 * D), BF16),
            sds((128, D), BF16),
            sds((512, D), BF16),
        ),
        in_specs=[vm] * 10 + [hbm] * 4,
        out_specs=(vm, vm, hbm, hbm, hbm, hbm),
        scratch_shapes=[
            pltpu.VMEM((KEYS, 128), jnp.int32),
            pltpu.VMEM((16, 128), F32),
            pltpu.VMEM((2, 8, 16, 128), F32),
            pltpu.VMEM((2, D, WQ), BF16),
            pltpu.VMEM((2, WO, D), BF16),
            pltpu.VMEM((2, D, W1), BF16),
            pltpu.VMEM((2, W1, D), BF16),
            pltpu.VMEM((2, TOK, D), BF16),
            pltpu.VMEM((2, TOK, D), BF16),
            pltpu.VMEM((2, TOK, W1), BF16),
            pltpu.VMEM((2, TOK, W1), F32),
            pltpu.VMEM((2, TOK, WQ), BF16),
            pltpu.VMEM((2, TOK, 2 * WO), BF16),
            pltpu.VMEM((2, TOK, WO), BF16),
            pltpu.VMEM((2, ROWS, D), F32),
            pltpu.VMEM((2, ROWS, D), F32),
            pltpu.VMEM((2, TOK, D), BF16),
            pltpu.VMEM((2, TOK, D), BF16),
            pltpu.VMEM((2, TOK, W1), BF16),
            pltpu.VMEM((2, TOK, WQ), BF16),
            pltpu.VMEM((TOK, WO), BF16),
            pltpu.VMEM((3, ROWS, D), BF16),
            pltpu.VMEM((4, 3, ROWS, D), BF16),
            pltpu.VMEM((ROWS, D), BF16),
            pltpu.VMEM((ROWS, D), BF16),
            pltpu.VMEM((ROWS, D), BF16),
            pltpu.VMEM((KEYS, 2 * WO), F32),
            pltpu.VMEM((2, TOK, 2 * WO), BF16),
            pltpu.VMEM((2, TOK, 2 * WO), BF16),
            pltpu.VMEM((ROWS, D), F32),
            pltpu.VMEM((ROWS, D), F32),
            pltpu.VMEM((CHIPS, 2, 128, WQ), BF16),
            pltpu.VMEM((CHIPS, 2, 128, W1), BF16),
            pltpu.VMEM((2, 128, D), BF16),
            pltpu.VMEM((2, 512, D), BF16),
            pltpu.VMEM((CHIPS, 128, WQ), BF16),
            pltpu.VMEM((CHIPS, 128, W1), BF16),
            pltpu.VMEM((128, D), BF16),
            pltpu.VMEM((512, D), BF16),
            pltpu.VMEM((2, REPL, CHIPS, 16, WQ), BF16),
            pltpu.VMEM((2, REPL, CHIPS, 16, W1), BF16),
            pltpu.VMEM((2, REPL, 16, D), BF16),
            pltpu.VMEM((2, REPL, 64, D), BF16),
            pltpu.VMEM((2, 8, D), F32),
            pltpu.VMEM((2, 128, D), F32),
            pltpu.VMEM((2, 64, WQ), F32),
            pltpu.VMEM((2, 16, D), F32),
            pltpu.VMEM((128, D), BF16),
            pltpu.VMEM((64, WQ), BF16),
            pltpu.VMEM((16, D), BF16),
            pltpu.VMEM((128, D), BF16),
            pltpu.VMEM((64, WQ), BF16),
            pltpu.VMEM((16, D), BF16),
            pltpu.VMEM((64, D), BF16),
            pltpu.VMEM((64, D), BF16),
            pltpu.VMEM((64, WQ), BF16),
            pltpu.VMEM((16, D), BF16),
            pltpu.VMEM((16, FF), BF16),
            pltpu.VMEM((64, WQ), BF16),
            pltpu.VMEM((16, 3 * D), BF16),
            pltpu.VMEM((REPL, 2, 8, D), F32),
            pltpu.VMEM((8, D), F32),
            pltpu.VMEM((8, D), F32),
            pltpu.VMEM((8, D), F32),
            dma((8, 2, CHIPS)),
            dma((8, 2, CHIPS)),
            dma((2, CHIPS)),
            dma((2, CHIPS)),
            dma((2,)),
            dma((2,)),
            dma((2,)),
            dma((2,)),
            dma((7, CHIPS)),
            dma((7, CHIPS)),
            dma((7, CHIPS)),
            dma((7, CHIPS)),
            dma((7, CHIPS)),
            dma((7, CHIPS)),
            dma((7, CHIPS)),
            dma((7, CHIPS)),
            dma((7,)),
            dma((2, 4)),
            dma((2, 4)),
            dma((2, 4, REPL)),
            dma((2, 4, REPL)),
            dma((4,)),
            dma((4,)),
            dma((4,)),
            dma((2, CHIPS)),
            dma((2, CHIPS)),
            dma((4, 4)),
            dma((4, 4)),
            dma((4, 4)),
            dma((4, 4)),
            dma((REPL,)),
            dma((REPL,)),
            dma((REPL,)),
            dma((REPL,)),
        ],
        compiler_params=pltpu.CompilerParams(
            collective_id=0, has_side_effects=True, vmem_limit_bytes=62 * 1024 * 1024
        ),
    )(*operands)


def body(
    boundary, image_of_token, ln1_gain, ln1_bias, w_qkv, qv_bias, w_out, out_bias,
    ln2_gain, ln2_bias, w_fc1, fc1_bias, w_fc2, fc2_bias,
):
    me = lax.axis_index("shard")
    x, c = me // 2, me % 2
    sec = lax.axis_index("section")
    bnd = boundary[0, :, 0]
    ids = lax.dynamic_index_in_dim(image_of_token[:, 0], sec, 0, keepdims=False).reshape(CHIPS, 2, ROWS)
    flipped = jnp.where(c == 0, ids, ids[:, ::-1])
    ids = jnp.swapaxes(flipped, 0, 1).reshape(KEYS)
    idr = jnp.broadcast_to(ids[None, :], (8, KEYS))
    edge, fv, f1, fa, fc, f2 = run_step(
        bnd, idr, ln1_gain, ln1_bias, qv_bias, out_bias, ln2_gain, ln2_bias, fc1_bias, fc2_bias,
        w_qkv[0], w_out[0], w_fc1[0], w_fc2[0],
    )
    g_qkv, g_fc1, g_out, g_fc2 = (v.astype(F32) for v in (fa, f1, fc, f2))

    whole = jnp.sum(fv, axis=0)
    pairs = jnp.sum(fv.reshape(CHIPS, 2, 8, D), axis=1)
    wide = jnp.concatenate(
        [whole[k] for k in (0, 1, 3, 4, 5, 7)]
        + [pairs[:, 2, :WO].reshape(-1), pairs[:, 2, WO : 2 * WO].reshape(-1), pairs[:, 6].reshape(-1)]
    )

    def part(at, size):
        return lax.dynamic_slice_in_dim(wide, at + me * size, size)[None]

    return (
        edge[None, :, None],
        part(0, 128),
        part(1024, 128),
        g_qkv[None],
        part(6 * D, 256),
        g_out[None],
        part(2 * D, 128),
        part(3 * D, 128),
        part(4 * D, 128),
        g_fc1[None],
        part(8 * D, 512),
        g_fc2[None],
        part(5 * D, 128),
    )


def solution(mesh):
    row = P("section", "shard")
    mat = P("section", "shard", None)
    edge = P("section", None, "replica", "shard", None)
    in_specs = (edge, P(None, "replica", None), row, row, mat, row, mat, row, row, row, mat, row, mat, row)
    out_specs = (edge, row, row, mat, row, mat, row, row, row, mat, row, mat, row)
    return jax.shard_map(body, mesh=mesh, in_specs=in_specs, out_specs=out_specs, check_vma=False)
```

time: 2030 us -> 350 us (0.17)
  waiting for transfers between devices: 1240 us -> 0 us
  blocking collectives: 447 us -> 0 us
  Pallas kernels: 0 us -> 338 us
  matrix products: 170 us -> 0 us
  local copies, waits for them, and re-layouts: 81 us -> 4.37 us
  other arithmetic: 58.5 us -> 6.58 us
    reduce_scatter x4 -> x0, waiting for transfers between devices: 962 us -> none  [the longest x1 366 us: body(): lax.psum_scatter(all_grads[10], ('shard', 'replica'), scatter_dimension=0...]
    pallas_call x0 -> x1, Pallas kernels: none -> 338 us  [run_step(): pl.pallas_call(step_kernel, out_shape=(sds((MICRO, ROWS, D), F32), sds((8...]
    unnamed x2 -> x0, blocking collectives: 302 us -> none
    all_gather x9 -> x0, waiting for transfers between devices: 188 us -> none  [the longest x1 42.3 us: body(): lax.all_gather(shards[10], 'shard', axis=0, tiled=True)]
    dot_general x47 -> x0, matrix products: 170 us -> none  [the longest x12 48.2 us: matmul_t(): lax.dot_general(first_op, second_op, (((1,), (1,)), ((), ())), preferred_...]
    all_gather x10 -> x0, blocking collectives: 145 us -> none  [the longest x1 38.2 us: body(): lax.all_gather(pieces[2].astype(jnp.bfloat16), 'replica', axis=0, tiled=T...]
    unnamed x19 -> x0, waiting for transfers between devices: 69.9 us -> none
    unnamed x406 -> x21, local copies, waits for them, and re-layouts: 39.3 us -> 1.6 us
  transfers between devices with their start and end apart: 20 -> 0, of which waited for: 17 -> 0; matrix products, arithmetic and copies ran while one was open for 6% -> 0% of each run, Pallas kernels for 0% -> 0%
where the time goes in v1:
time: 350 us
  Pallas kernels  338 us (97%)
  other arithmetic  6.58 us (2%)
  local copies, waits for them, and re-layouts  4.37 us (1%)
    pallas_call x1, Pallas kernels, run_step(): pl.pallas_call(step_kernel, out_shape=(sds((MICRO, ROWS, D), F32), sds((8...  338 us

profile of v1, /device:TPU:0, one launch (start us, length us, event | category | flops | bytes accessed | tf_op | source)
XLA Modules:
  0.0 349.6 jit_solution(11749205497677092708)
XLA Ops:
  0.6 0.0 copy-start
  0.7 0.7 copy-done
  1.4 0.1 reshape.36
  1.5 0.1 broadcast_in_dim.58
  1.6 0.6 broadcast_in_dim.59.idr
  2.2 337.8 %shard_map.237 = (f32[2,96,1024]{2,1,0:T(8,128)}, f32[8,8,1024]{2,1,0:T(8,128)}, bf16[128,4096]{1,0:T(8,128)(2,1)}, bf16[128,3072]{1,0:T(8,128)(2,1)}, bf16[128,...) custom-call(bf16[2,96,1024]{2,1,0:T(8,128)(2,1)} %bitcast.51, s32[8,768]{1,0:T(8,128)} %broadcast_in_dim.59.idr, ...), custom_call_target="tpu_custom_call" | custom-call | tf_op jit(solution)/shard_map/pallas_call | solution.py:840
  340.0 0.0 copy-start.1
  340.0 2.9 bitcast_convert_fusion
  342.9 0.0 copy-start.4
  342.9 0.0 copy-done.1
  342.9 0.0 copy-start.2
  342.9 1.5 bitcast_convert_fusion.1
  344.4 0.0 copy-start.5
  344.4 0.0 copy-start.3
  344.4 0.0 copy-done.4
  344.4 1.3 bitcast_convert_fusion.2
  345.7 0.0 copy-done.2
  346.0 0.6 dynamic-slice_bitcast_fusion
  346.6 0.7 dynamic_slice.35
  347.2 0.6 dynamic_slice.31
  347.9 0.0 copy-done.5
  347.9 0.8 bitcast_convert_fusion.3
  348.7 0.0 copy-done.3
  348.7 0.9 copy.40
  (18 shorter events, 0.2 us)
Async XLA Ops:
  0.6 0.7 copy-start
  340.0 2.9 copy-start.1
  342.9 1.5 copy-start.4
  342.9 2.8 copy-start.2
  344.4 3.4 copy-start.5
  344.4 4.3 %copy-start.3 = (f32[2,96,1024]{2,1,0:T(8,128)S(1)}, f32[2,96,1024]{2,1,0:T(8,128)}, u32[]{:S(2)}) copy-start(f32[2,96,1024]{2,1,0:T(8,128)} %get-tuple-element.19) | copy-start | bytes 2359300

commit v2 on v1

--- a/solution.py
+++ b/solution.py
@@ -81,7 +81,7 @@
     pga, pgb, pgc, pgd, rga, rgb, rgc, rgd, lga, lgb, lgc, lgd,
     vg_o, em, ea, ec, zm, za, zc, ym, ya, yc, pm, p2, pa, pc, q1, qt, qa, lv, tv, zv, yv,
     xs_sem, xr_sem, ks_sem, kr_sem, ds_sem, dr_sem, cs_sem, cr_sem,
-    wxs, wxr, wns, wnr, was, war, wfs, wfr, loc_sem, ps_sem, pr_sem, rs_sem, rr_sem, out_sem,
+    wxs, wxr, wns, wnr, was, war, wfs, wfr, wys, wyr, loc_sem, ps_sem, pr_sem, rs_sem, rr_sem, out_sem,
     zs_sem, zr_sem, as_sem, ar_sem, hs_sem, hr_sem, ys_sem, yr_sem, vs_sem, vr_sem, us_sem, ur_sem,
 ):
     sec = lax.axis_index("section")
@@ -150,9 +150,38 @@
         dst = w_dst(sec, kind, peer(4 - d), core)
         return copy_to(own_piece(kind, d), dst, wns.at[kind, d], wnr.at[kind, d], mate)
 
-    def across_copy(kind, d, layer):
-        dst = w_dst(layer, kind, peer(4 - d), c)
-        return copy_to(own_piece(kind, d), dst, was.at[kind, d], war.at[kind, d], across_to)
+    yi = lax.rem(rep, 2)
+    y_mate = {"replica": flip(rep)}
+
+    def half_src(kind, h):
+        if kind == 0:
+            return vec_s
+        size = 256 if kind == 4 else 64
+        rows = pl.ds(pl.multiple_of(h * size, size), size)
+        if kind in QKV:
+            return wq_s.at[rows, pl.ds(pl.multiple_of(QKV[kind] * D + x * WO, WO), WO)]
+        if kind == 2:
+            return w1_s.at[rows, pl.ds(pl.multiple_of(x * W1, W1), W1)]
+        return (wo_s if kind == 3 else w2_s).at[rows]
+
+    def half_dst(layer, kind, d, h):
+        chip = peer(4 - d)
+        if kind == 0:
+            return w_dst(layer, kind, chip, c)
+        size = 256 if kind == 4 else 64
+        base = c if kind in (3, 4) else chip * 2 + c
+        rows = pl.ds(pl.multiple_of((base * 2 + h) * size, size), size)
+        if kind in QKV:
+            return wq.at[layer, rows, pl.ds(QKV[kind] * WO, WO)]
+        return {2: w1, 3: wo, 4: w2}[kind].at[layer, rows]
+
+    def across_copy(kind, d, layer, h):
+        src = half_src(kind, h) if d == 0 else half_dst(sec, kind, d, h)
+        return copy_to(src, half_dst(layer, kind, d, h), was.at[kind, d], war.at[kind, d], across_to)
+
+    def pass_copy(kind, d, h):
+        ref = half_dst(1 - sec, kind, d, h)
+        return copy_to(ref, ref, wys.at[kind, d], wyr.at[kind, d], y_mate)
 
     def far_copy(kind, d, core):
         ref = w_dst(1 - sec, kind, peer(4 - d), core)
@@ -166,22 +195,31 @@
             for d in (1, 3, 2):
                 x_copy(kind, d, x).start()
         near_copy(kind, 0, c).start()
+        across_copy(kind, 0, sec, yi).start()
         local_copy(kind).start()
 
     def settle_near(kind):
-        across_copy(kind, 0, sec).start()
         for d in kinds[kind][1:]:
             x_copy(kind, d, peer(4 - d)).wait_recv()
             near_copy(kind, d, c).start()
-            across_copy(kind, d, sec).start()
+            across_copy(kind, d, sec, yi).start()
         local_copy(kind).wait()
         for d in kinds[kind]:
             near_copy(kind, d, 1 - c).wait_recv()
 
-    def settle_far(kind):
+    def far_in(kind):
         for d in kinds[kind]:
-            across_copy(kind, d, 1 - sec).wait_recv()
+            across_copy(kind, d, 1 - sec, 1 - yi).wait_recv()
+            if kind != 0:
+                pass_copy(kind, d, 1 - yi).start()
+
+    def far_on(kind):
+        for d in kinds[kind]:
+            if kind != 0:
+                pass_copy(kind, d, yi).wait_recv()
             far_copy(kind, d, c).start()
+
+    def far_done(kind):
         for d in kinds[kind]:
             far_copy(kind, d, 1 - c).wait_recv()
 
@@ -199,16 +237,17 @@
         launch(kind)
     idc[...] = jnp.transpose(jnp.broadcast_to(idr[:1, :], (128, KEYS)))
     settle_near(0)
-    settle_far(0)
-    swap_copy.wait_recv()
 
     @pl.when(sec == 0)
     def _():
         rin[0] = bnd[0].astype(F32)
-        gnext[...] = swap[...].astype(F32)
 
     @pl.when(sec == 1)
     def _():
+        far_in(0)
+        far_on(0)
+        far_done(0)
+        swap_copy.wait_recv()
         rin[0] = swap[...].astype(F32)
         gnext[...] = bnd[1].astype(F32)
 
@@ -267,7 +306,8 @@
     lane = lax.broadcasted_iota(jnp.int32, (1, 128), 1)
 
     def forward(l, first):
-        need_far = l + sec == 1
+        lower = (l == 0) & (sec == 0)
+        upper = (l == 0) & (sec == 1)
         qkv_b = jnp.concatenate(
             pieces(l, x, (2, 3)) + [jnp.zeros((1, WO), F32)] + pieces(l, 4 + x, (2, 3)), axis=1
         )
@@ -286,10 +326,11 @@
             launch(2)
             launch(4)
 
-        @pl.when(need_far)
-        def _():
-            for kind in QKV:
-                settle_far(kind)
+        @pl.when(upper)
+        def _():
+            for step in (far_in, far_on, far_done):
+                for kind in QKV:
+                    step(kind)
 
         def project(k, _):
             d = gray(k)
@@ -308,11 +349,12 @@
         @pl.when(l == 0)
         def _():
             settle_near(3)
-            settle_near(2)
-
-        @pl.when(need_far)
-        def _():
-            settle_far(3)
+
+        @pl.when(upper)
+        def _():
+            far_in(3)
+            far_on(3)
+            far_done(3)
 
         for d in range(CHIPS):
             kv_copy(l, d).wait_recv()
@@ -333,13 +375,24 @@
                     qm = jnp.where(lane // HEAD == half, q, jnp.zeros_like(q))
                     s = jnp.concatenate([mm_t(qm, k_own), mm_t(qm, k_par)], axis=1) + bias
                     p = jnp.exp(s - jnp.max(s, axis=1, keepdims=True))
-                    p = (p / jnp.sum(p, axis=1, keepdims=True)).astype(BF16)
-                    outs.append(mm(p[:, :TOK], v_own) + mm(p[:, TOK:], v_par))
+                    scale = 1.0 / jnp.sum(p, axis=1, keepdims=True)
+                    p = p.astype(BF16)
+                    outs.append((mm(p[:, :TOK], v_own) + mm(p[:, TOK:], v_par)) * scale)
                 wt[l, rows, lanes] = jnp.where(lane < HEAD, outs[0], outs[1]).astype(BF16)
             send_part(RS1, l, d, mm(wt[l, rows], wo[l]))
             return 0
 
         lax.fori_loop(0, CHIPS, attend, 0)
+
+        @pl.when(l == 0)
+        def _():
+            settle_near(2)
+
+        @pl.when(upper)
+        def _():
+            far_in(2)
+            far_in(4)
+
         rmid[l] = rin[l] + (scatter_add(RS1, l, own[...]) + vec_row(l, 4))
         normed, _ = norm_parts(rmid[l])
         n2[l, rows_of(x)] = (normed * vec_row(l, 5) + vec_row(l, 6)).astype(BF16)
@@ -349,10 +402,18 @@
         def _():
             settle_near(4)
 
-        @pl.when(need_far)
-        def _():
-            settle_far(2)
-            settle_far(4)
+        @pl.when(upper)
+        def _():
+            for step in (far_on, far_done):
+                step(2)
+                step(4)
+
+        @pl.when(lower)
+        def _():
+            swap_copy.wait_recv()
+            gnext[...] = swap[...].astype(F32)
+            for kind in (0, 1, 5, 6, 3, 2, 4):
+                far_in(kind)
 
         def feed(k, _):
             d = gray(k)
@@ -371,6 +432,13 @@
             return 0
 
         lax.fori_loop(0, CHIPS, feed, 0)
+
+        @pl.when(lower)
+        def _():
+            for step in (far_on, far_done):
+                for kind in (0, 1, 5, 6, 3, 2, 4):
+                    step(kind)
+
         out = rmid[l] + (scatter_add(RS2, l, own[...]) + vec_row(l, 11))
 
         @pl.when(l == 0)
@@ -711,8 +779,6 @@
             turn_copy(n, d, peer(4 - d)).wait_recv()
 
     zi = rep // 2
-    yi = lax.rem(rep, 2)
-    y_mate = {"replica": flip(rep)}
     pieces_of = ((q1, f1), (qa, fa), (pc, fc), (p2, f2))
 
     def slot_ref(n, slot):
@@ -725,6 +791,11 @@
         src = pieces_of[n][0]
         where = {"replica": lax.rem(zi + d, 4) * 2 + yi}
         return copy_to(src, slot_ref(n, slot), hs_sem.at[n, d], hr_sem.at[n, d], where)
+
+    def along_z_late(n, d, slot):
+        ref = slot_ref(n, slot)
+        where = {"replica": lax.rem(zi + d, 4) * 2 + yi}
+        return copy_to(ref, ref, hs_sem.at[n, 4 + d], hr_sem.at[n, 4 + d], where)
 
     def along_y(n, d, y):
         dst = slot_ref(n, slot_of(d, y))
@@ -740,6 +811,11 @@
         keep_piece(n).start()
 
     def share_on(n):
+        if n in (2, 3):
+            along_y(n, 0, 1 - yi).wait_recv()
+            for d in (1, 3, 2):
+                along_z_late(n, d, flip(rep)).start()
+            return
         for d in (1, 3, 2):
             along_z(n, d, slot_of(d, yi)).wait_recv()
             along_y(n, d, yi).start()
@@ -763,6 +839,7 @@
     share_start(3)
     turn_wait(0)
     share_start(0)
+    share_on(3)
     collect_att(0)
     za[...] = ea[1 - sec].astype(BF16)
     zc[...] = ec[1 - sec].astype(BF16)
@@ -785,13 +862,17 @@
             at = t * D + chip * WO
             qa[:, at : at + WO] = qt[chip * 16 : chip * 16 + 16, t * WO : t * WO + WO]
     share_start(1)
-    share_on(3)
     share_on(0)
     share_on(2)
     share_on(1)
     for n in range(4):
-        for d in range(4):
-            along_y(n, d, 1 - yi).wait_recv()
+        if n in (2, 3):
+            for d in (1, 3, 2):
+                along_z(n, d, slot_of(d, yi)).wait_recv()
+                along_z_late(n, d, slot_of(d, 1 - yi)).wait_recv()
+        else:
+            for d in range(4):
+                along_y(n, d, 1 - yi).wait_recv()
         keep_piece(n).wait()
     for j in range(1, REPL):
         vec_share(j, lax.rem(me + 8 - j, 8)).wait_recv()
@@ -805,7 +886,9 @@
             if d != 0:
                 x_copy(kind, d, x).wait_send()
             near_copy(kind, d, c).wait_send()
-            across_copy(kind, d, sec).wait_send()
+            across_copy(kind, d, sec, yi).wait_send()
+            if kind != 0:
+                pass_copy(kind, d, 1 - yi).wait_send()
             far_copy(kind, d, c).wait_send()
     for l in range(2):
         for d in (1, 2, 3):
@@ -825,7 +908,9 @@
     for n in range(4):
         for d in (1, 2, 3):
             along_z(n, d, rep).wait_send()
-        for d in range(4):
+            if n in (2, 3):
+                along_z_late(n, d, flip(rep)).wait_send()
+        for d in range(1 if n in (2, 3) else 4):
             along_y(n, d, yi).wait_send()
     for j in range(1, REPL):
         vec_copy(j).wait_send()
@@ -930,6 +1015,8 @@
             dma((7, CHIPS)),
             dma((7, CHIPS)),
             dma((7, CHIPS)),
+            dma((7, CHIPS)),
+            dma((7, CHIPS)),
             dma((7,)),
             dma((2, 4)),
             dma((2, 4)),
@@ -940,8 +1027,8 @@
             dma((4,)),
             dma((2, CHIPS)),
             dma((2, CHIPS)),
-            dma((4, 4)),
-            dma((4, 4)),
+            dma((4, 8)),
+            dma((4, 8)),
             dma((4, 4)),
             dma((4, 4)),
             dma((REPL,)),

time: 350 us -> 328 us (0.937)
  Pallas kernels: 338 us -> 315 us
    pallas_call x1, Pallas kernels: 338 us -> 315 us  [run_step(): pl.pallas_call(step_kernel, out_shape=(sds((MICRO, ROWS, D), F32), sds((8...]
where the time goes in v2:
time: 328 us; the launch traced here: 326 us
  Pallas kernels  315 us (96%)
  other arithmetic  6.58 us (2%)
  local copies, waits for them, and re-layouts  4.37 us (1%)
    pallas_call x1, Pallas kernels, run_step(): pl.pallas_call(step_kernel, out_shape=(sds((MICRO, ROWS, D), F32), sds((8...  315 us

profile of v2, /device:TPU:0, one launch (start us, length us, event | category | flops | bytes accessed | tf_op | source)
XLA Modules:
  0.0 326.4 jit_solution(17801313112145722197)
XLA Ops:
  0.6 0.0 copy-start
  0.7 0.7 copy-done
  1.4 0.1 reshape.36
  1.5 0.1 broadcast_in_dim.58
  1.6 0.6 broadcast_in_dim.59.idr
  2.2 314.7 %shard_map.237 = (f32[2,96,1024]{2,1,0:T(8,128)}, f32[8,8,1024]{2,1,0:T(8,128)}, bf16[128,4096]{1,0:T(8,128)(2,1)}, bf16[128,3072]{1,0:T(8,128)(2,1)}, bf16[128,...) custom-call(bf16[2,96,1024]{2,1,0:T(8,128)(2,1)} %bitcast.51, s32[8,768]{1,0:T(8,128)} %broadcast_in_dim.59.idr, ...), custom_call_target="tpu_custom_call" | custom-call | tf_op jit(solution)/shard_map/pallas_call | solution.py:925
  316.8 0.0 copy-start.1
  316.9 2.9 bitcast_convert_fusion
  319.7 0.0 copy-start.4
  319.7 0.0 copy-done.1
  319.7 0.0 copy-start.2
  319.7 1.5 bitcast_convert_fusion.1
  321.3 0.0 copy-start.5
  321.3 0.0 copy-start.3
  321.3 0.0 copy-done.4
  321.3 1.3 bitcast_convert_fusion.2
  322.6 0.0 copy-done.2
  322.8 0.6 dynamic-slice_bitcast_fusion
  323.4 0.7 dynamic_slice.35
  324.1 0.6 dynamic_slice.31
  324.7 0.0 copy-done.5
  324.7 0.8 bitcast_convert_fusion.3
  325.5 0.0 copy-done.3
  325.5 0.9 copy.40
  (18 shorter events, 0.2 us)
Async XLA Ops:
  0.6 0.7 copy-start
  316.8 2.9 copy-start.1
  319.7 1.5 copy-start.4
  319.7 2.8 copy-start.2
  321.3 3.4 %copy-start.5 = (bf16[128,1024]{1,0:T(8,128)(2,1)S(1)}, bf16[128,1024]{1,0:T(8,128)(2,1)}, u32[]{:S(2)}) copy-start(bf16[128,1024]{1,0:T(8,128)(2,1)} %get-tuple-element.22) | copy-start | bytes 786436
  321.3 4.3 %copy-start.3 = (f32[2,96,1024]{2,1,0:T(8,128)S(1)}, f32[2,96,1024]{2,1,0:T(8,128)}, u32[]{:S(2)}) copy-start(f32[2,96,1024]{2,1,0:T(8,128)} %get-tuple-element.19) | copy-start | bytes 2359300

commit v3 on v2

--- a/solution.py
+++ b/solution.py
@@ -74,12 +74,12 @@
 
 def step_kernel(
     bnd, idr, v_ln1g, v_ln1b, v_qv, v_out, v_ln2g, v_ln2b, v_fc1, v_fc2, wq_s, wo_s, w1_s, w2_s,
-    edge_o, fv, f1, fa, fc, f2,
-    idc, vec_s, vecs, wq, wo, w1, w2,
+    edge_o, vo, f1, fa, fc, f2,
+    fv, idc, vec_s, vecs, wq, wo, w1, w2,
     n1, n2, act, dgl, qkv, kvp, wt, rin, rmid, g, ga, dh, dp, dw,
     stage, landed, swap, carry_s, carry_r, dkv, dkv_s, dkv_r, own, gnext,
     pga, pgb, pgc, pgd, rga, rgb, rgc, rgd, lga, lgb, lgc, lgd,
-    vg_o, em, ea, ec, zm, za, zc, ym, ya, yc, pm, p2, pa, pc, q1, qt, qa, lv, tv, zv, yv,
+    vg_o, em, ea, ec, zm, za, zc, ym, ya, yc, pm, p2, pa, pc, q1, qt, qa, lv, tv, zv, yv, zv_sum,
     xs_sem, xr_sem, ks_sem, kr_sem, ds_sem, dr_sem, cs_sem, cr_sem,
     wxs, wxr, wns, wnr, was, war, wfs, wfr, wys, wyr, loc_sem, ps_sem, pr_sem, rs_sem, rr_sem, out_sem,
     zs_sem, zr_sem, as_sem, ar_sem, hs_sem, hr_sem, ys_sem, yr_sem, vs_sem, vr_sem, us_sem, ur_sem,
@@ -370,15 +370,15 @@
                 v_own = qkv[l, :, 2 * WO + pair * 128 : 2 * WO + pair * 128 + 128]
                 k_par = kvp[l, :, lanes]
                 v_par = kvp[l, :, WO + pair * 128 : WO + pair * 128 + 128]
-                outs = []
-                for half in range(2):
-                    qm = jnp.where(lane // HEAD == half, q, jnp.zeros_like(q))
-                    s = jnp.concatenate([mm_t(qm, k_own), mm_t(qm, k_par)], axis=1) + bias
-                    p = jnp.exp(s - jnp.max(s, axis=1, keepdims=True))
-                    scale = 1.0 / jnp.sum(p, axis=1, keepdims=True)
-                    p = p.astype(BF16)
-                    outs.append((mm(p[:, :TOK], v_own) + mm(p[:, TOK:], v_par)) * scale)
-                wt[l, rows, lanes] = jnp.where(lane < HEAD, outs[0], outs[1]).astype(BF16)
+                low_q = jnp.where(lane < HEAD, q, jnp.zeros_like(q))
+                qs = jnp.concatenate([low_q, jnp.where(lane < HEAD, jnp.zeros_like(q), q)], axis=0)
+                s = jnp.concatenate([mm_t(qs, k_own), mm_t(qs, k_par)], axis=1)
+                s = s.reshape(2, ROWS, KEYS) + bias[None]
+                p = jnp.exp(s - jnp.max(s, axis=2, keepdims=True))
+                scale = (1.0 / jnp.sum(p, axis=2, keepdims=True)).reshape(2 * ROWS, 1)
+                p = p.reshape(2 * ROWS, KEYS).astype(BF16)
+                out = (mm(p[:, :TOK], v_own) + mm(p[:, TOK:], v_par)) * scale
+                wt[l, rows, lanes] = jnp.where(lane < HEAD, out[:ROWS], out[ROWS:]).astype(BF16)
             send_part(RS1, l, d, mm(wt[l, rows], wo[l]))
             return 0
 
@@ -675,20 +675,18 @@
                     ],
                     axis=0,
                 )
-                dqs = []
-                for half in range(2):
-                    keep = lane // HEAD == half
-                    qm = jnp.where(keep, q, jnp.zeros_like(q))
-                    dom = jnp.where(keep, do, jnp.zeros_like(do))
-                    s = mm_t(k_all, qm) + bias
-                    p = jnp.exp(s - jnp.max(s, axis=0, keepdims=True))
-                    p = p * (1.0 / jnp.sum(p, axis=0, keepdims=True))
-                    dpr = mm_t(v_all, dom)
-                    ds = (p * (dpr - jnp.sum(p * dpr, axis=0, keepdims=True))).astype(BF16)
-                    dkv[:, lanes] += mm(ds, qm)
-                    dkv[:, WO + pair * 128 : WO + pair * 128 + 128] += mm(p.astype(BF16), dom)
-                    dqs.append(over_rows(ds, k_all))
-                dq = jnp.where(lane < HEAD, dqs[0], dqs[1]) * (HEAD**-0.5)
+                none = jnp.zeros_like(q)
+                qs = jnp.concatenate([jnp.where(lane < HEAD, q, none), jnp.where(lane < HEAD, none, q)], axis=0)
+                dos = jnp.concatenate([jnp.where(lane < HEAD, do, none), jnp.where(lane < HEAD, none, do)], axis=0)
+                s = mm_t(k_all, qs) + jnp.concatenate([bias, bias], axis=1)
+                p = jnp.exp(s - jnp.max(s, axis=0, keepdims=True))
+                p = p * (1.0 / jnp.sum(p, axis=0, keepdims=True))
+                dpr = mm_t(v_all, dos)
+                ds = (p * (dpr - jnp.sum(p * dpr, axis=0, keepdims=True))).astype(BF16)
+                dkv[:, lanes] += mm(ds, qs)
+                dkv[:, WO + pair * 128 : WO + pair * 128 + 128] += mm(p.astype(BF16), dos)
+                dq = over_rows(ds, k_all)
+                dq = jnp.where(lane < HEAD, dq[:128], dq[128:]) * (HEAD**-0.5)
                 dp[l, rows, lanes] = dq.astype(BF16)
             return 0
 
@@ -876,6 +874,18 @@
         keep_piece(n).wait()
     for j in range(1, REPL):
         vec_share(j, lax.rem(me + 8 - j, 8)).wait_recv()
+    total = fv[0]
+    for n in range(1, 8):
+        total = total + fv[n]
+    zv_sum[...] = total
+    mine = pl.ds(pl.multiple_of(me * 128, 128), 128)
+    for row, k in ((0, 0), (1, 1), (4, 3), (5, 4), (6, 5), (11, 7)):
+        vo[row : row + 1, :] = zv_sum[k : k + 1, mine]
+    for row, k, chip, base, t in [(2, 2, lax.rem(me, 4), me // 4 * 256, t) for t in range(2)] + [
+        (7, 6, x, c * 512, t) for t in range(4)
+    ]:
+        cols = pl.ds(pl.multiple_of(base + t * 128, 128), 128)
+        vo[row + t : row + t + 1, :] = fv[2 * chip, k : k + 1, cols] + fv[2 * chip + 1, k : k + 1, cols]
 
     carry_copy.wait_recv()
     edge_o[1 - sec] = carry_r[...].astype(F32)
@@ -926,7 +936,7 @@
         step_kernel,
         out_shape=(
             sds((MICRO, ROWS, D), F32),
-            sds((8, 8, D), F32),
+            sds((16, 128), F32),
             sds((128, FF), BF16),
             sds((128, 3 * D), BF16),
             sds((128, D), BF16),
@@ -935,6 +945,7 @@
         in_specs=[vm] * 10 + [hbm] * 4,
         out_specs=(vm, vm, hbm, hbm, hbm, hbm),
         scratch_shapes=[
+            pltpu.VMEM((8, 8, D), F32),
             pltpu.VMEM((KEYS, 128), jnp.int32),
             pltpu.VMEM((16, 128), F32),
             pltpu.VMEM((2, 8, 16, 128), F32),
@@ -999,6 +1010,7 @@
             pltpu.VMEM((8, D), F32),
             pltpu.VMEM((8, D), F32),
             pltpu.VMEM((8, D), F32),
+            pltpu.VMEM((8, D), F32),
             dma((8, 2, CHIPS)),
             dma((8, 2, CHIPS)),
             dma((2, CHIPS)),
@@ -1037,7 +1049,7 @@
             dma((REPL,)),
         ],
         compiler_params=pltpu.CompilerParams(
-            collective_id=0, has_side_effects=True, vmem_limit_bytes=62 * 1024 * 1024
+            collective_id=0, has_side_effects=True, vmem_limit_bytes=63 * 1024 * 1024
         ),
     )(*operands)
 
@@ -1054,36 +1066,29 @@
     flipped = jnp.where(c == 0, ids, ids[:, ::-1])
     ids = jnp.swapaxes(flipped, 0, 1).reshape(KEYS)
     idr = jnp.broadcast_to(ids[None, :], (8, KEYS))
-    edge, fv, f1, fa, fc, f2 = run_step(
+    edge, vo, f1, fa, fc, f2 = run_step(
         bnd, idr, ln1_gain, ln1_bias, qv_bias, out_bias, ln2_gain, ln2_bias, fc1_bias, fc2_bias,
         w_qkv[0], w_out[0], w_fc1[0], w_fc2[0],
     )
     g_qkv, g_fc1, g_out, g_fc2 = (v.astype(F32) for v in (fa, f1, fc, f2))
 
-    whole = jnp.sum(fv, axis=0)
-    pairs = jnp.sum(fv.reshape(CHIPS, 2, 8, D), axis=1)
-    wide = jnp.concatenate(
-        [whole[k] for k in (0, 1, 3, 4, 5, 7)]
-        + [pairs[:, 2, :WO].reshape(-1), pairs[:, 2, WO : 2 * WO].reshape(-1), pairs[:, 6].reshape(-1)]
-    )
-
-    def part(at, size):
-        return lax.dynamic_slice_in_dim(wide, at + me * size, size)[None]
+    def part(at, count):
+        return vo[at : at + count].reshape(1, count * 128)
 
     return (
         edge[None, :, None],
-        part(0, 128),
-        part(1024, 128),
+        part(0, 1),
+        part(1, 1),
         g_qkv[None],
-        part(6 * D, 256),
+        part(2, 2),
         g_out[None],
-        part(2 * D, 128),
-        part(3 * D, 128),
-        part(4 * D, 128),
+        part(4, 1),
+        part(5, 1),
+        part(6, 1),
         g_fc1[None],
-        part(8 * D, 512),
+        part(7, 4),
         g_fc2[None],
-        part(5 * D, 128),
+        part(11, 1),
     )
 
 

time: 328 us -> 324 us (0.988)
  Pallas kernels: 315 us -> 310 us
    pallas_call x1, Pallas kernels: 315 us -> 310 us  [run_step(): pl.pallas_call(step_kernel, out_shape=(sds((MICRO, ROWS, D), F32), sds((1...]
where the time goes in v3:
time: 324 us; the launch traced here: 321 us
  Pallas kernels  310 us (96%)
  other arithmetic  6.55 us (2%)
  local copies, waits for them, and re-layouts  4.08 us (1%)
    pallas_call x1, Pallas kernels, run_step(): pl.pallas_call(step_kernel, out_shape=(sds((MICRO, ROWS, D), F32), sds((1...  310 us

profile of v3, /device:TPU:0, one launch (start us, length us, event | category | flops | bytes accessed | tf_op | source)
XLA Modules:
  0.0 321.0 jit_solution(11491953507507404205)
XLA Ops:
  0.6 0.0 copy-start
  0.7 0.7 copy-done
  1.4 0.1 reshape.39
  1.5 0.1 broadcast_in_dim.34
  1.6 0.6 broadcast_in_dim.35.idr
  2.2 309.7 %shard_map.237 = (f32[2,96,1024]{2,1,0:T(8,128)}, f32[16,128]{1,0:T(8,128)}, bf16[128,4096]{1,0:T(8,128)(2,1)}, bf16[128,3072]{1,0:T(8,128)(2,1)}, bf16[128,1024]{1,0:T(8,128)(2,1)}, /*index=5*/bf16[512,1024]{1,0:T(8,128)(2,1)}) custom-call(bf16[2,96,1024]{2,1,0:T(8,128)(2,1)} %bitcast.28, s32[8,768]{1,0:T(8,128)} %broadcast_in_dim.35.idr, ...), custom_call_target="tpu_custom_call" | custom-call | tf_op jit(solution)/shard_map/pallas_call | solution.py:935
  311.9 0.0 copy-start.1
  311.9 2.9 bitcast_convert_fusion
  314.8 0.0 copy-start.3
  314.8 0.0 copy-done.1
  314.8 0.0 copy-start.4
  314.8 1.5 bitcast_convert_fusion.1
  316.3 0.0 copy-start.5
  316.3 0.0 copy-start.2
  316.3 0.0 copy-done.3
  316.3 1.3 bitcast_convert_fusion.2
  317.6 0.0 copy-done.4
  317.6 0.8 bitcast_convert_fusion.3
  318.5 0.0 copy-done.5
  318.5 0.5 fusion
  319.0 0.6 slice.30
  319.6 0.6 slice.26
  320.1 0.0 copy-done.2
  320.1 0.9 copy.32
  (4 shorter events, 0.1 us)
Async XLA Ops:
  0.6 0.7 copy-start
  311.9 2.9 copy-start.1
  314.8 1.5 copy-start.3
  314.8 2.8 copy-start.4
  316.3 2.2 copy-start.5
  316.3 3.8 %copy-start.2 = (f32[2,96,1024]{2,1,0:T(8,128)S(1)}, f32[2,96,1024]{2,1,0:T(8,128)}, u32[]{:S(2)}) copy-start(f32[2,96,1024]{2,1,0:T(8,128)} %get-tuple-element.19) | copy-start | bytes 2359300

commit v4 on v3

--- a/solution.py
+++ b/solution.py
@@ -580,6 +580,10 @@
         for j in range(1, REPL):
             total = total + lgc[l, j].astype(F32)
         ec[l] = total
+
+    def cross_copy(n):
+        src, dst = ((zm, ym), (za, ya), (zc, yc), (zv, yv))[n]
+        return copy_to(src, dst, zs_sem.at[n], zr_sem.at[n], across_to)
 
     def backward(i, first):
         l = 1 - i
@@ -726,6 +730,9 @@
         @pl.when(i == 1)
         def _():
             spread_att(0)
+            collect_mlp(0)
+            zm[...] = em[1 - sec].astype(BF16)
+            cross_copy(0).start()
 
         dn1 = scatter_add(BRS2, l, own[...])
         d_in = rmid[l] + norm_back(rin[l], vec_row(l, 0), dn1, 0)
@@ -752,10 +759,6 @@
 
     def vec_share(j, slot):
         return copy_to(tv, fv.at[slot], us_sem.at[j], ur_sem.at[j], at_shard(j))
-
-    def cross_copy(n):
-        src, dst = ((zm, ym), (za, ya), (zc, yc), (zv, yv))[n]
-        return copy_to(src, dst, zs_sem.at[n], zr_sem.at[n], across_to)
 
     def turn_refs(n, source):
         if n == 0:
@@ -820,9 +823,13 @@
 
     for j in range(1, REPL):
         vec_copy(j).start()
-    collect_mlp(0)
-    zm[...] = em[1 - sec].astype(BF16)
-    cross_copy(0).start()
+    cross_copy(0).wait_recv()
+    pm[...] = (em[sec, :64] + ym[:64].astype(F32)).astype(BF16)
+    p2[...] = (em[sec, 64:] + ym[64:].astype(F32)).astype(BF16)
+    turn_start(0)
+    share_start(3)
+    turn_wait(0)
+    share_start(0)
     total = vg_o[...]
     for j in range(1, REPL):
         vec_copy(j).wait_recv()
@@ -830,13 +837,6 @@
     vg_o_sum = total
     zv[...] = jnp.where(sec == 0, vg_o_sum[1], vg_o_sum[0])
     cross_copy(3).start()
-    cross_copy(0).wait_recv()
-    pm[...] = (em[sec, :64] + ym[:64].astype(F32)).astype(BF16)
-    p2[...] = (em[sec, 64:] + ym[64:].astype(F32)).astype(BF16)
-    turn_start(0)
-    share_start(3)
-    turn_wait(0)
-    share_start(0)
     share_on(3)
     collect_att(0)
     za[...] = ea[1 - sec].astype(BF16)

time: 324 us -> 316 us (0.975)
  Pallas kernels: 310 us -> 305 us
    pallas_call x1, Pallas kernels: 310 us -> 305 us  [run_step(): pl.pallas_call(step_kernel, out_shape=(sds((MICRO, ROWS, D), F32), sds((1...]
where the time goes in v4:
time: 316 us
  Pallas kernels  305 us (97%)
  other arithmetic  6.55 us (2%)
  local copies, waits for them, and re-layouts  4.08 us (1%)
    pallas_call x1, Pallas kernels, run_step(): pl.pallas_call(step_kernel, out_shape=(sds((MICRO, ROWS, D), F32), sds((1...  305 us

profile of v4, /device:TPU:0, one launch (start us, length us, event | category | flops | bytes accessed | tf_op | source)
XLA Modules:
  0.0 315.8 jit_solution(13692748052066554551)
XLA Ops:
  0.6 0.0 copy-start
  0.7 0.7 copy-done
  1.4 0.1 reshape.39
  1.5 0.1 broadcast_in_dim.34
  1.6 0.6 broadcast_in_dim.35.idr
  2.2 304.5 %shard_map.237 = (f32[2,96,1024]{2,1,0:T(8,128)}, f32[16,128]{1,0:T(8,128)}, bf16[128,4096]{1,0:T(8,128)(2,1)}, bf16[128,3072]{1,0:T(8,128)(2,1)}, bf16[128,1024]{1,0:T(8,128)(2,1)}, /*index=5*/bf16[512,1024]{1,0:T(8,128)(2,1)}) custom-call(bf16[2,96,1024]{2,1,0:T(8,128)(2,1)} %bitcast.28, s32[8,768]{1,0:T(8,128)} %broadcast_in_dim.35.idr, ...), custom_call_target="tpu_custom_call" | custom-call | tf_op jit(solution)/shard_map/pallas_call | solution.py:935
  306.7 0.0 copy-start.1
  306.7 2.9 bitcast_convert_fusion
  309.6 0.0 copy-start.3
  309.6 0.0 copy-done.1
  309.6 0.0 copy-start.4
  309.6 1.5 bitcast_convert_fusion.1
  311.1 0.0 copy-start.5
  311.1 0.0 copy-start.2
  311.1 0.0 copy-done.3
  311.1 1.3 bitcast_convert_fusion.2
  312.4 0.0 copy-done.4
  312.4 0.8 bitcast_convert_fusion.3
  313.3 0.0 copy-done.5
  313.3 0.5 fusion
  313.8 0.6 slice.30
  314.4 0.6 slice.26
  315.0 0.0 copy-done.2
  315.0 0.9 copy.32
  (4 shorter events, 0.1 us)
Async XLA Ops:
  0.6 0.7 copy-start
  306.7 2.9 copy-start.1
  309.6 1.5 copy-start.3
  309.6 2.8 copy-start.4
  311.1 2.2 copy-start.5
  311.1 3.8 %copy-start.2 = (f32[2,96,1024]{2,1,0:T(8,128)S(1)}, f32[2,96,1024]{2,1,0:T(8,128)}, u32[]{:S(2)}) copy-start(f32[2,96,1024]{2,1,0:T(8,128)} %get-tuple-element.19) | copy-start | bytes 2359300
